TPU v7x, 256 devices: a whole 4x4x8 slice. The times are simulated.
256 devices in a mesh: dp: 16 (over y_hi, z), expert: 16 (over y_lo, x, core).
Axes of the slice: x: 4, y: 4 (y_hi: 2, y_lo: 2; y = y_hi * 2 + y_lo), z: 8, core: 2. Of those that a mesh axis runs over, the one named last changes fastest.
Arguments:
- tokens: bfloat16 [2048, 196, 1024], P(('dp', 'expert')), may hold values from -4 to 4
- norm_gain: float32 [1024], replicated, may hold values from 0.1 to 1.9
- slot_weight: bfloat16 [1024, 16], replicated, may hold values from -2.0507812 to 2.0507812
- w_in: bfloat16 [16, 1024, 2048], P('expert', None, 'dp'), may hold values from -0.1875 to 0.1875
- w_out: bfloat16 [16, 2048, 1024], P('expert', 'dp'), may hold values from -0.125 to 0.125
- cotangent: bfloat16 [2048, 196, 1024], P(('dp', 'expert')), may hold values from -6 to 6
Outputs:
- d_tokens: bfloat16 [2048, 196, 1024], P(('dp', 'expert'))
- d_slot_weight: float32 [1024, 16], replicated
- d_gain: float32 [1024], replicated
- d_w_in: float32 [16, 1024, 2048], P('expert', None, 'dp')
- d_w_out: float32 [16, 2048, 1024], P('expert', 'dp')
All inputs are finite; a program needn't handle non-finite values.
Results may differ from a plain program's by a relative error of at most 0.019.
The roundings to bfloat16 on the way count: a program that leaves them out, or rounds other values in their place, can miss the bound.
Values may be sent and summed in bfloat16 or wider, within the bound.
No kernel may reach another device: no remote copies, remote signals or barrier semaphores. Data moves between devices by JAX's collectives and lax.ppermute only.
A program may use at most 128 MiB of HBM per device.

v0:
```python
import jax
import jax.numpy as jnp
from jax import lax
from jax.sharding import PartitionSpec as P

eps = 1e-06


def normalize(tokens, norm_gain):
    as_float = tokens.astype(jnp.float32)
    token_mean = jnp.mean(as_float, axis=-1, keepdims=True)
    centred = as_float - token_mean
    inv_std = lax.rsqrt(jnp.mean(centred * centred, axis=-1, keepdims=True) + eps)
    x_hat = centred * inv_std
    normed = (x_hat * norm_gain).astype(jnp.bfloat16)
    return (normed, x_hat, inv_std)


def on_device(tokens, norm_gain, slot_weight, w_in, w_out, cotangent):
    features = tokens.shape[2]
    normed, x_hat, inv_std = normalize(tokens, norm_gain)
    logits = jnp.einsum("btd,ds->bts", normed, slot_weight, preferred_element_type=jnp.float32)
    p_dispatch = jax.nn.softmax(logits, axis=1)
    p_combine = jax.nn.softmax(logits, axis=2)
    dispatch = p_dispatch.astype(jnp.bfloat16)
    combine = p_combine.astype(jnp.bfloat16)
    slots = jnp.einsum("bts,btd->sbd", dispatch, normed, preferred_element_type=jnp.float32).astype(
        jnp.bfloat16
    )
    cot_slots = jnp.einsum(
        "bts,btd->sbd", combine, cotangent, preferred_element_type=jnp.float32
    ).astype(jnp.bfloat16)
    got_slots, got_cot = (
        lax.all_to_all(slots, "expert", split_axis=0, concat_axis=0, tiled=True),
        lax.all_to_all(cot_slots, "expert", split_axis=0, concat_axis=0, tiled=True),
    )
    slot_shape = got_slots.shape
    slot_rows = got_slots.reshape(-1, features)
    cot_rows = got_cot.reshape(-1, features)
    first_part = w_in[0]
    second_part = w_out[0]
    first_layer = lax.all_gather(first_part, "dp", axis=1, tiled=True)
    second_layer = lax.all_gather(second_part, "dp", axis=0, tiled=True)
    pre_act = jnp.dot(slot_rows, first_layer, preferred_element_type=jnp.float32)
    hidden_f, gelu_back = jax.vjp(jax.nn.gelu, pre_act)
    hidden = hidden_f.astype(jnp.bfloat16)
    y_rows = jnp.dot(hidden, second_layer, preferred_element_type=jnp.float32).astype(jnp.bfloat16)
    d_hidden = jnp.dot(cot_rows, second_layer.T, preferred_element_type=jnp.float32)
    d_act = gelu_back(d_hidden)[0].astype(jnp.bfloat16)
    slot_grad = jnp.dot(d_act, first_layer.T, preferred_element_type=jnp.float32).astype(
        jnp.bfloat16
    )
    d_second = lax.psum_scatter(
        jnp.dot(hidden.T, cot_rows, preferred_element_type=jnp.float32).astype(jnp.bfloat16),
        "dp",
        scatter_dimension=0,
        tiled=True,
    ).astype(jnp.float32)
    d_first_full = jnp.dot(slot_rows.T, d_act, preferred_element_type=jnp.float32)
    d_first = lax.psum_scatter(
        d_first_full.astype(jnp.bfloat16), "dp", scatter_dimension=1, tiled=True
    ).astype(jnp.float32)
    out_slots, grad_slots = (
        lax.all_to_all(
            y_rows.reshape(slot_shape), "expert", split_axis=0, concat_axis=0, tiled=True
        ),
        lax.all_to_all(
            slot_grad.reshape(slot_shape), "expert", split_axis=0, concat_axis=0, tiled=True
        ),
    )
    d_combine = jnp.einsum("btd,sbd->bts", cotangent, out_slots, preferred_element_type=jnp.float32)
    d_dispatch = jnp.einsum("sbd,btd->bts", grad_slots, normed, preferred_element_type=jnp.float32)
    from_combine = p_combine * (d_combine - jnp.sum(p_combine * d_combine, axis=2, keepdims=True))
    from_dispatch = p_dispatch * (
        d_dispatch - jnp.sum(p_dispatch * d_dispatch, axis=1, keepdims=True)
    )
    d_logits = (from_combine + from_dispatch).astype(jnp.bfloat16)
    d_normed = jnp.einsum("bts,sbd->btd", dispatch, grad_slots, preferred_element_type=jnp.float32)
    d_normed = d_normed + jnp.einsum(
        "bts,ds->btd", d_logits, slot_weight, preferred_element_type=jnp.float32
    )
    weight_part = jnp.einsum("btd,bts->ds", normed, d_logits, preferred_element_type=jnp.float32)
    gain_part = jnp.sum(d_normed * x_hat, axis=(0, 1))
    scaled = d_normed * norm_gain
    d_tokens = inv_std * (
        scaled
        - jnp.mean(scaled, axis=-1, keepdims=True)
        - x_hat * jnp.mean(scaled * x_hat, axis=-1, keepdims=True)
    )
    d_slot_weight, d_gain = lax.psum((weight_part, gain_part), ("dp", "expert"))
    return (d_tokens.astype(jnp.bfloat16), d_slot_weight, d_gain, d_first[None], d_second[None])


def solution(mesh):
    placed = (
        P(("dp", "expert"), None, None),
        P(),
        P(),
        P("expert", None, "dp"),
        P("expert", "dp", None),
        P(("dp", "expert"), None, None),
    )
    return jax.shard_map(
        on_device,
        mesh=mesh,
        in_specs=placed,
        out_specs=(
            P(("dp", "expert"), None, None),
            P(),
            P(),
            P("expert", None, "dp"),
            P("expert", "dp", None),
        ),
        check_vma=False,
    )
```

profile of v0, /device:TPU:1, one launch (start us, length us, event | category | flops | bytes accessed | tf_op | source)
XLA Modules:
  0.0 903.1 jit_solution(8301676818304080405)
XLA Ops:
  8.7 5.3 convert_reduce_fusion
  14.0 5.0 fusion.16
  19.1 4.4 fusion.86
  24.2 6.7 fusion.44
  30.9 1.8 copy.28
  32.7 7.0 all-to-all-start.1
  41.3 5.2 fusion.45
  48.4 5.7 all-to-all-start
  54.1 62.1 %all-gather.7.cloned.1.call-done = bf16[1,1024,2048]{2,1,0:T(8,128)(2,1)} async-done(((bf16[1,1024,128]{2,1,0:T(8,128)(2,1)}), bf16[1,1024,2048]{2,1,0:T(8,128)(2,1)}) %all-gather.7.cloned.1.call-update) | async-done | bytes 4194320 | tf_op jit(solution)/shard_map/all_gather | solution.py:42
  116.3 3.9 fusion.19
  120.1 95.4 %all-gather.5.cloned.1.call-done = bf16[1,2048,1024]{2,1,0:T(8,128)(2,1)} async-done(((bf16[1,128,1024]{2,1,0:T(8,128)(2,1)}), bf16[1,2048,1024]{2,1,0:T(8,128)(2,1)}) %all-gather.5.cloned.1.call-update) | async-done | bytes 4194320 | tf_op jit(solution)/shard_map/all_gather | solution.py:43
  215.6 4.4 fusion.68
  220.8 3.3 convolution_convert_fusion.1
  224.1 6.4 copy.34
  230.6 4.6 convolution_convert_fusion
  235.2 4.1 fusion.41
  239.3 8.5 all-to-all-start.3
  247.8 4.6 fusion.38
  252.4 2.5 all-to-all-done.3
  255.6 4.7 all-to-all-start.2
  260.4 2.9 fusion.57
  265.0 2.7 all-to-all-done.2
  267.7 5.0 fusion.80
  272.6 5.1 fusion.61
  277.7 12.3 %fusion.15 = (f32[1024]{0:T(1024)S(1)}, f32[8,196]{1,0:T(8,128)S(1)}, f32[8,196]{1,0:T(8,128)S(1)}, f32[8,196,1024]{2,1,0:T(8,128)}) fusion(f32[8,196]{1,0:T(8,128)S(1)} %add_rsqrt_fusion, f32[8,196]{1,0:T(8,128)S(1)} %broadcast_multiply_fusion.2, bf16[8,196,1024]{2,0,1:T(8,128)(2,1)} %param.6, f32[1024]{0:T(1024)S(1)} %copy-done.8, ...), kind=kOutput, calls=%fused_computation.17 | convolution fusion | flops 67507968 | bytes 16452608 | tf_op jit(solution)/shard_map/bts,sbd->btd/dot_general | solution.py:78
  290.0 6.0 fusion.14
  296.0 3.5 copy.33
  299.4 74.6 %psum.15 = f32[1024]{0:T(1024)} all-reduce(f32[1024]{0:T(1024)S(1)} %get-tuple-element.20), channel_id=1, replica_groups=mesh['dp'=16,'expert'=16] {'dp','expert'}, use_global_device_ids=true, to_apply=%region_12.0 | all-reduce | flops 1024 | bytes 8192 | tf_op jit(solution)/shard_map/psum | solution.py:90
  374.0 6.6 convolution_bitcast_fusion
  380.6 56.7 %reduce-scatter.7.cloned.1.call-done = bf16[128,1024]{1,0:T(8,128)(2,1)} async-done(((bf16[2048,1024]{1,0:T(8,128)(2,1)}), bf16[128,1024]{1,0:T(8,128)(2,1)}) %reduce-scatter.7.cloned.1.call-update) | async-done | bytes 262160
  439.3 209.1 %reduce-scatter.5.cloned.1.call-done = bf16[128,1024]{1,0:T(8,128)(2,1)} async-done(((bf16[2048,1024]{1,0:T(8,128)(2,1)}), bf16[128,1024]{1,0:T(8,128)(2,1)}) %reduce-scatter.5.cloned.1.call-update) | async-done | bytes 262160 | tf_op jit(solution)/shard_map/reduce_scatter | solution.py:53
  650.2 244.7 %all-reduce.2.cloned.1.call-done = f32[1024,16]{0,1:T(8,128)} async-done(((f32[1024,16]{0,1:T(8,128)}), f32[1024,16]{0,1:T(8,128)}) %all-reduce.2.cloned.1.call-update) | async-done | bytes 65552 | tf_op jit(solution)/shard_map/psum | solution.py:90
  (41 shorter events, 14.3 us)
Async XLA Ops:
  7.2 34.2 %copy-start = (bf16[8,196,1024]{2,0,1:T(8,128)(2,1)S(1)}, bf16[8,196,1024]{2,0,1:T(8,128)(2,1)}, u32[]{:S(2)}) copy-start(bf16[8,196,1024]{2,0,1:T(8,128)(2,1)} %param.11) | copy-start | bytes 9633796
  7.2 11.9 %copy-start.8 = (f32[1024]{0:T(1024)S(1)}, f32[1024]{0:T(1024)}, u32[]{:S(2)}) copy-start(f32[1024]{0:T(1024)} %param.7) | copy-start | bytes 12292
  7.2 11.9 %copy-start.7 = (bf16[1024,16]{0,1:T(8,128)(2,1)S(1)}, bf16[1024,16]{0,1:T(8,128)(2,1)}, u32[]{:S(2)}) copy-start(bf16[1024,16]{0,1:T(8,128)(2,1)} %param.8) | copy-start | bytes 98308
  7.2 109.1 %all-gather.7.cloned.1.call-start = ((), (), s32[]{:S(2)}) async-start(), calls=%async_computation.9 | async-start | bytes 4456448 | tf_op jit(solution)/shard_map/all_gather | solution.py:42
  7.9 207.6 %all-gather.5.cloned.1.call-start = ((), (), s32[]{:S(2)}) async-start(), calls=%async_computation.8 | async-start | bytes 4456448 | tf_op jit(solution)/shard_map/all_gather | solution.py:43
  23.5 9.3 %copy-start.2 = (f32[8,196,16]{1,2,0:T(8,128)}, f32[8,196,16]{1,2,0:T(8,128)S(1)}, u32[]{:S(2)}) copy-start(f32[8,196,16]{1,2,0:T(8,128)S(1)} %fusion.86) | copy-start | bytes 301060
  32.7 15.7 %all-to-all-start.1 = ((bf16[16,8,1024]{2,1,0:T(8,128)(2,1)}), bf16[16,8,1024]{2,1,0:T(8,128)(2,1)S(1)}, u32[]{:S(2)}, u32[]{:S(2)}) async-start(bf16[16,8,1024]{2,1,0:T(8,128)(2,1)} %copy.28), calls=%async_computation.1 | async-start | bytes 524288 | tf_op jit(solution)/shard_map/all_to_all | solution.py:34
  48.4 71.8 %all-to-all-start = ((bf16[16,8,1024]{2,1,0:T(8,128)(2,1)}), bf16[16,8,1024]{2,1,0:T(8,128)(2,1)}, u32[]{:S(2)}, u32[]{:S(2)}) async-start(bf16[16,8,1024]{2,1,0:T(8,128)(2,1)} %copy.27), calls=%async_computation | async-start | bytes 524288 | tf_op jit(solution)/shard_map/all_to_all | solution.py:35
  54.1 383.3 %reduce-scatter.7.cloned.1.call-start = ((), (), s32[]{:S(2)}) async-start(), calls=%async_computation.10 | async-start | bytes 4456448
  220.0 0.8 copy-start.1
  230.5 417.9 %reduce-scatter.5.cloned.1.call-start = ((), (), s32[]{:S(2)}) async-start(), calls=%async_computation.7 | async-start | bytes 4456448 | tf_op jit(solution)/shard_map/reduce_scatter | solution.py:53
  239.3 15.5 %all-to-all-start.3 = ((bf16[16,8,1024]{2,1,0:T(8,128)(2,1)}), bf16[16,8,1024]{2,1,0:T(8,128)(2,1)S(1)}, u32[]{:S(2)}, u32[]{:S(2)}) async-start(bf16[16,8,1024]{2,1,0:T(8,128)(2,1)} %fusion.41), calls=%async_computation.3 | async-start | bytes 524288 | tf_op jit(solution)/shard_map/all_to_all | solution.py:64
  254.9 0.7 copy-start.5
  255.6 12.1 %all-to-all-start.2 = ((bf16[16,8,1024]{2,1,0:T(8,128)(2,1)}), bf16[16,8,1024]{2,1,0:T(8,128)(2,1)}, u32[]{:S(2)}, u32[]{:S(2)}) async-start(bf16[16,8,1024]{2,1,0:T(8,128)(2,1)} %fusion.38), calls=%async_computation.2 | async-start | bytes 524288 | tf_op jit(solution)/shard_map/all_to_all | solution.py:67
  260.3 12.3 %copy-start.4 = (f32[8,196,16]{1,2,0:T(8,128)S(1)}, f32[8,196,16]{1,2,0:T(8,128)}, u32[]{:S(2)}) copy-start(f32[8,196,16]{1,2,0:T(8,128)} %get-tuple-element.24) | copy-start | bytes 301060
  260.3 634.6 %all-reduce.2.cloned.1.call-start = ((), (), s32[]{:S(2)}) async-start(), calls=%async_computation.6 | async-start | bytes 131072 | tf_op jit(solution)/shard_map/psum | solution.py:90
  265.0 12.8 %copy-start.3 = (f32[8,196,16]{1,2,0:T(8,128)S(1)}, f32[8,196,16]{1,2,0:T(8,128)}, u32[]{:S(2)}) copy-start(f32[8,196,16]{1,2,0:T(8,128)} %copy-done.2) | copy-start | bytes 301060
  290.0 84.0 %copy-start.6 = (f32[8,196,16]{1,2,0:T(8,128)S(1)}, f32[8,196,16]{1,2,0:T(8,128)}, u32[]{:S(2)}) copy-start(f32[8,196,16]{1,2,0:T(8,128)} %fusion.56) | copy-start | bytes 301060
Sparse Core Ops, SparseCore 0:
  10.5 105.7 all-gather.6
  118.8 96.6 all-gather.4
  230.7 206.6 reduce-scatter.6
  441.8 206.6 reduce-scatter.4
  654.4 240.5 all-reduce.1
where the time goes:
time: 912 us; the launch traced here: 903 us
  waiting for transfers between devices  675 us (74%)
  blocking collectives  74.6 us (8%)
  matrix products  73 us (8%)
  starting transfers between devices  26.1 us (3%)
  other arithmetic  23.1 us (3%)
  local copies, waits for them, and re-layouts  17.6 us (2%)
  between operations  14.1 us (2%)
    psum x1, waiting for transfers between devices, on_device(): d_slot_weight, d_gain = lax.psum((weight_part, gain_part), ('dp', 'expert'))  245 us
    reduce_scatter x1, waiting for transfers between devices, on_device(): lax.psum_scatter(jnp.dot(hidden.T, cot_rows, preferred_element_type=jnp.f...  209 us
    all_gather x1, waiting for transfers between devices, on_device(): second_layer = lax.all_gather(second_part, 'dp', axis=0, tiled=True)  95.4 us
    psum x1, blocking collectives, on_device(): d_slot_weight, d_gain = lax.psum((weight_part, gain_part), ('dp', 'expert'))  74.6 us
    all_gather x1, waiting for transfers between devices, on_device(): first_layer = lax.all_gather(first_part, 'dp', axis=1, tiled=True)  62.1 us
    unnamed x6, waiting for transfers between devices  58.2 us
  transfers between devices with their start and end apart: 9, of which 7 were waited for; matrix products, arithmetic and copies ran while one was open for 11% of the time, Pallas kernels for 0%

commit v1 on v0

v1 whole, which is shorter than its diff:
```python
import jax
import jax.numpy as jnp
from jax import lax
from jax.experimental import pallas as pl
from jax.experimental.pallas import tpu as pltpu
from jax.sharding import Mesh
from jax.sharding import PartitionSpec as P

eps = 1e-06
f32 = jnp.float32
bf16 = jnp.bfloat16
VMEM = 40 * 1024 * 1024


def dot(a, b, ca, cb):
    return lax.dot_general(a, b, (((ca,), (cb,)), ((), ())), preferred_element_type=f32)


def front_kernel(
    x_ref, c_ref, gain_ref, wrep_ref, out_ref, normed_ref, pd_ref, pc_ref, lg_ref, st_ref, acc_s, acc_c
):
    b = pl.program_id(0)
    images = pl.num_programs(0)
    slots, rows, features = out_ref.shape[1:]
    x = x_ref[0].astype(f32)
    mu = jnp.mean(x, axis=-1, keepdims=True)
    xc = x - mu
    inv = lax.rsqrt(jnp.mean(xc * xc, axis=-1, keepdims=True) + eps)
    normed = (xc * inv * gain_ref[...]).astype(bf16)
    normed_ref[0] = normed
    logits = dot(normed, wrep_ref[...], 1, 0)
    lane = lax.broadcasted_iota(jnp.int32, logits.shape, 1)
    mine = lax.rem(lane, rows // 2) == b
    ed = jnp.exp(logits - jnp.max(logits, axis=0, keepdims=True))
    pd = jnp.where(mine, ed / jnp.sum(ed, axis=0, keepdims=True), 0.0)
    ec = jnp.where(mine, jnp.exp(logits - jnp.max(logits, axis=1, keepdims=True)), 0.0)
    pc = ec / jnp.sum(ec, axis=1, keepdims=True)
    pd_ref[0] = pd
    pc_ref[0] = pc
    lg_ref[0] = logits
    st_ref[0] = jnp.where(lane == 0, mu, inv)

    @pl.when(b == 0)
    def _():
        acc_s[...] = jnp.zeros_like(acc_s)
        acc_c[...] = jnp.zeros_like(acc_c)

    acc_s[...] += dot(pd.astype(bf16), normed, 0, 0)
    acc_c[...] += dot(pc.astype(bf16), c_ref[0], 0, 0)

    @pl.when(b == images - 1)
    def _():
        both = jnp.concatenate(
            [
                acc_s[...].reshape(slots, rows // 2, features),
                acc_c[...].reshape(slots, rows // 2, features),
            ],
            axis=1,
        ).astype(bf16)
        for copy in range(out_ref.shape[0]):
            out_ref[copy] = both


def front(tokens, norm_gain, wrep, cotangent, copies):
    images, tok, features = tokens.shape
    wide = wrep.shape[1]
    slots = wide // images
    image = pl.BlockSpec((1, tok, features), lambda b: (b, 0, 0))
    narrow = pl.BlockSpec((1, tok, wide), lambda b: (b, 0, 0))
    routing = jax.ShapeDtypeStruct((images, tok, wide), f32)
    return pl.pallas_call(
        front_kernel,
        grid=(images,),
        in_specs=[
            image,
            image,
            pl.BlockSpec((1, features), lambda b: (0, 0)),
            pl.BlockSpec((features, wide), lambda b: (0, 0)),
        ],
        out_specs=[
            pl.BlockSpec((copies, slots, 2 * images, features), lambda b: (0, 0, 0, 0)),
            image,
            narrow,
            narrow,
            narrow,
            narrow,
        ],
        out_shape=[
            jax.ShapeDtypeStruct((copies, slots, 2 * images, features), bf16),
            jax.ShapeDtypeStruct((images, tok, features), bf16),
            routing,
            routing,
            routing,
            routing,
        ],
        scratch_shapes=[pltpu.VMEM((wide, features), f32)] * 2,
        compiler_params=pltpu.CompilerParams(vmem_limit_bytes=VMEM),
        cost_estimate=pl.CostEstimate(flops=4 * 10**9, bytes_accessed=14 * 2**20, transcendentals=10**6),
        name="front",
    )(tokens, cotangent, norm_gain, wrep)


gelu_c = 0.7978845608028654
gelu_k = 0.044715


def expert_kernel(act_ref, w_ref, ret_ref, dw_ref, slot_s, cot_s, y_acc, g_acc):
    p = pl.program_id(0)
    peers, rows, features = act_ref.shape
    half = rows // 2
    pair, _, part = w_ref.shape

    @pl.when(p == 0)
    def _():
        act = act_ref[...].astype(f32)
        slot_s[...] = act[:, :half].reshape(peers * half, features).astype(bf16)
        cot_s[...] = act[:, half:].reshape(peers * half, features).astype(bf16)
        y_acc[...] = jnp.zeros_like(y_acc)
        g_acc[...] = jnp.zeros_like(g_acc)

    slots = slot_s[...]
    cots = cot_s[...]
    w1 = jnp.concatenate([w_ref[q, :features] for q in range(pair)], axis=1)
    w2 = jnp.concatenate(
        [
            jnp.concatenate([w_ref[q, pl.ds(features + j * part, part)] for q in range(pair)], axis=0)
            for j in range(features // part)
        ],
        axis=1,
    )
    pre = dot(slots, w1, 1, 0)
    sq = pre * pre
    th = jnp.tanh(gelu_c * (pre + gelu_k * (sq * pre)))
    cdf = 0.5 * (1.0 + th)
    hidden = (pre * cdf).astype(bf16)
    slope = cdf + 0.5 * pre * (1.0 - th * th) * (gelu_c * (1.0 + 3.0 * gelu_k * sq))
    d_act = (dot(cots, w2, 1, 1) * slope).astype(bf16)
    y_acc[...] += dot(hidden, w2, 1, 0)
    g_acc[...] += dot(d_act, w1, 1, 1)
    d_w1 = dot(slots, d_act, 0, 0).astype(bf16)
    d_w2 = dot(hidden, cots, 0, 0).astype(bf16)
    for q in range(pair):
        mine = slice(q * part, (q + 1) * part)
        dw_ref[q, :features] = d_w1[:, mine]
        for j in range(features // part):
            dw_ref[q, pl.ds(features + j * part, part)] = d_w2[mine, j * part : (j + 1) * part]

    @pl.when(p == pl.num_programs(0) - 1)
    def _():
        ret_ref[...] = jnp.concatenate(
            [
                y_acc[...].reshape(peers, half, features),
                g_acc[...].reshape(peers, half, features),
            ],
            axis=1,
        ).astype(bf16)


def expert(act, weights):
    peers, rows, features = act.shape
    parts, long, part = weights.shape
    all_rows = peers * rows // 2
    pair = 2
    whole = pl.BlockSpec((peers, rows, features), lambda p: (0, 0, 0))
    block = pl.BlockSpec((pair, long, part), lambda p: (p, 0, 0))
    return pl.pallas_call(
        expert_kernel,
        grid=(parts // pair,),
        in_specs=[whole, block],
        out_specs=[whole, block],
        out_shape=[
            jax.ShapeDtypeStruct((peers, rows, features), bf16),
            jax.ShapeDtypeStruct((parts, long, part), bf16),
        ],
        scratch_shapes=[
            pltpu.VMEM((all_rows, features), bf16),
            pltpu.VMEM((all_rows, features), bf16),
            pltpu.VMEM((all_rows, features), f32),
            pltpu.VMEM((all_rows, features), f32),
        ],
        compiler_params=pltpu.CompilerParams(vmem_limit_bytes=VMEM),
        cost_estimate=pl.CostEstimate(flops=4 * 10**9, bytes_accessed=10 * 2**20, transcendentals=10**6),
        name="expert",
    )(act, weights)


def back_kernel(
    x_ref, c_ref, normed_ref, pd_ref, pc_ref, lg_ref, st_ref, gain_ref, wrep_t_ref, ret_ref,
    dt_ref, sums_ref, out_s, grad_s, means_s, acc,
):
    b = pl.program_id(0)
    copies, slots, rows, features = ret_ref.shape
    half = rows // 2
    wide = slots * half
    gain = gain_ref[...]

    @pl.when(b == 0)
    def _():
        total = ret_ref[0].astype(f32)
        for copy in range(1, copies):
            total = total + ret_ref[copy].astype(f32)
        out_s[...] = total[:, :half].reshape(wide, features).astype(bf16)
        grad_s[:wide] = total[:, half:].reshape(wide, features).astype(bf16)
        grad_s[wide:] = wrep_t_ref[...]
        means_s[...] = lax.dot_general(
            jnp.broadcast_to(gain, (8, features)),
            grad_s[...].astype(f32),
            (((1,), (1,)), ((), ())),
            preferred_element_type=f32,
            precision=lax.Precision.HIGHEST,
        ) * (1.0 / features)
        acc[...] = jnp.zeros_like(acc)

    normed = normed_ref[0]
    pd = pd_ref[0]
    pc = pc_ref[0]
    d_combine = dot(c_ref[0], out_s[...], 1, 1)
    d_dispatch = dot(normed, grad_s[:wide], 1, 1)
    from_combine = pc * (d_combine - jnp.sum(pc * d_combine, axis=1, keepdims=True))
    from_dispatch = pd * (d_dispatch - jnp.sum(pd * d_dispatch, axis=0, keepdims=True))
    d_logits = (from_combine + from_dispatch).astype(bf16)
    dispatch = pd.astype(bf16)
    coef = jnp.concatenate([dispatch, d_logits], axis=1)
    mean_dot = jnp.sum(
        dispatch.astype(f32) * d_dispatch + d_logits.astype(f32) * lg_ref[0], axis=1, keepdims=True
    ) * (1.0 / features)
    mean_scaled = jnp.sum(coef.astype(f32) * means_s[0:1], axis=1, keepdims=True)
    d_normed = dot(coef, grad_s[...], 1, 0)
    acc[...] += dot(coef, normed, 0, 0)
    mu = st_ref[0, :, 0:1]
    inv = st_ref[0, :, 1:2]
    dt_ref[0] = (
        inv * (d_normed * gain - mean_scaled) - (x_ref[0].astype(f32) - mu) * (inv * inv * mean_dot)
    ).astype(bf16)

    @pl.when(b == pl.num_programs(0) - 1)
    def _():
        d_weight = jnp.sum(acc[wide:].reshape(slots, half, features), axis=1)
        d_gain = jnp.sum(acc[...] * grad_s[...].astype(f32), axis=0, keepdims=True) / gain
        part = sums_ref.shape[2]
        for j in range(features // part):
            cols = slice(j * part, (j + 1) * part)
            sums_ref[j, :slots] = d_weight[:, cols]
            sums_ref[j, slots:] = jnp.broadcast_to(d_gain[:, cols], (8, part))


def back(tokens, cotangent, normed, pd, pc, lg, st, norm_gain, wrep_t, ret, pieces):
    images, tok, features = tokens.shape
    wide = wrep_t.shape[0]
    slots = wide // images
    image = pl.BlockSpec((1, tok, features), lambda b: (b, 0, 0))
    narrow = pl.BlockSpec((1, tok, wide), lambda b: (b, 0, 0))
    sums = (pieces, slots + 8, features // pieces)
    return pl.pallas_call(
        back_kernel,
        grid=(images,),
        in_specs=[
            image,
            image,
            image,
            narrow,
            narrow,
            narrow,
            narrow,
            pl.BlockSpec((1, features), lambda b: (0, 0)),
            pl.BlockSpec((wide, features), lambda b: (0, 0)),
            pl.BlockSpec(ret.shape, lambda b: (0, 0, 0, 0)),
        ],
        out_specs=[image, pl.BlockSpec(sums, lambda b: (0, 0, 0))],
        out_shape=[
            jax.ShapeDtypeStruct((images, tok, features), bf16),
            jax.ShapeDtypeStruct(sums, f32),
        ],
        scratch_shapes=[
            pltpu.VMEM((wide, features), bf16),
            pltpu.VMEM((2 * wide, features), bf16),
            pltpu.VMEM((8, 2 * wide), f32),
            pltpu.VMEM((2 * wide, features), f32),
        ],
        compiler_params=pltpu.CompilerParams(vmem_limit_bytes=VMEM),
        cost_estimate=pl.CostEstimate(flops=6 * 10**9, bytes_accessed=18 * 2**20, transcendentals=0),
        name="back",
    )(tokens, cotangent, normed, pd, pc, lg, st, norm_gain, wrep_t, ret)


def on_device(tokens, norm_gain, slot_weight, w_in, w_out, cotangent):
    images, _, features = tokens.shape
    slots = slot_weight.shape[1]
    part = w_in.shape[2]
    pieces = features // part
    halves = lax.axis_size("yh")
    peers = ("yh", "expert")

    second = w_out[0].reshape(part, pieces, part).swapaxes(0, 1).reshape(features, part)
    weights = lax.all_gather(jnp.concatenate([w_in[0], second], axis=0), "z", axis=0, tiled=False)

    gain = norm_gain[None]
    wrep = jnp.repeat(slot_weight, images, axis=1)
    sent, normed, pd, pc, lg, st = front(tokens, gain, wrep, cotangent, halves)
    act = lax.all_to_all(
        sent.reshape(halves * slots, 2 * images, features), peers, 0, 0, tiled=True
    )
    ret, d_w = expert(act, weights)
    d_w = lax.psum_scatter(d_w, "z", scatter_dimension=0, tiled=False).astype(f32)
    ret = lax.all_to_all(ret, peers, 0, 0, tiled=True)
    d_tokens, sums = back(
        tokens, cotangent, normed, pd, pc, lg, st, gain, wrep.T,
        ret.reshape(halves, slots, 2 * images, features), lax.axis_size("z"),
    )
    sums = jnp.sum(lax.all_to_all(sums, "z", 0, 0, tiled=True), axis=0)
    n_peers = halves * lax.axis_size("expert")
    sums = jnp.sum(
        lax.all_to_all(jnp.broadcast_to(sums[None], (n_peers, *sums.shape)), peers, 0, 0, tiled=True), axis=0
    )
    n_z = lax.axis_size("z")
    sums = lax.all_to_all(jnp.broadcast_to(sums[None], (n_z, *sums.shape)), "z", 0, 0, tiled=True)
    d_slot_weight = sums[:, :slots].swapaxes(1, 2).reshape(features, slots)
    d_gain = sums[:, slots].reshape(features)
    d_first = d_w[:features]
    d_second = d_w[features:].reshape(pieces, part, part).swapaxes(0, 1).reshape(part, features)
    return (d_tokens, d_slot_weight, d_gain, d_first[None], d_second[None])


def solution(mesh):
    dp = mesh.shape["dp"]
    fine = Mesh(mesh.devices.reshape(2, dp // 2, mesh.shape["expert"]), ("yh", "z", "expert"))
    everywhere = P(("yh", "z", "expert"), None, None)
    first = P("expert", None, ("yh", "z"))
    second = P("expert", ("yh", "z"), None)
    return jax.shard_map(
        on_device,
        mesh=fine,
        in_specs=(everywhere, P(), P(), first, second, everywhere),
        out_specs=(everywhere, P(), P(), first, second),
        check_vma=False,
    )
```

time: 912 us -> 176 us (0.19)
  waiting for transfers between devices: 675 us -> 14.2 us
  matrix products: 73 us -> 0 us
  Pallas kernels: 0 us -> 23.7 us
  starting transfers between devices: 26.1 us -> 3.62 us
  other arithmetic: 23.1 us -> 1.83 us
  local copies, waits for them, and re-layouts: 17.6 us -> 38.6 us
    psum x1 -> x0, waiting for transfers between devices: 245 us -> none  [on_device(): d_slot_weight, d_gain = lax.psum((weight_part, gain_part), ('dp', 'expert'))]
    reduce_scatter x1, waiting for transfers between devices: 209 us -> 0.01 us  [on_device(): lax.psum_scatter(d_w, 'z', scatter_dimension=0, tiled=False).astype(f32)]
    all_gather x2 -> x1, waiting for transfers between devices: 158 us -> 12.3 us  [on_device(): lax.all_gather(jnp.concatenate([w_in[0], second], axis=0), 'z', axis=0, t...]
    all_to_all x0 -> x4, blocking collectives: none -> 78.4 us  [the longest x1 25.7 us: on_device(): lax.all_to_all(sent.reshape(halves * slots, 2 * images, features), peers,...]
    psum x1 -> x0, blocking collectives: 74.6 us -> none  [on_device(): d_slot_weight, d_gain = lax.psum((weight_part, gain_part), ('dp', 'expert'))]
    dot_general x14 -> x0, matrix products: 73 us -> none  [the longest x1 12.3 us: on_device(): jnp.einsum('bts,sbd->btd', dispatch, grad_slots, preferred_element_type=j...]
    unnamed x6 -> x2, waiting for transfers between devices: 58.2 us -> 0.03 us
    pallas_call x0 -> x3, Pallas kernels: none -> 23.7 us  [the longest x1 10.4 us: back(): pl.pallas_call(back_kernel, grid=(images,), in_specs=[image, image, image...]
  transfers between devices with their start and end apart: 9 -> 3, of which waited for: 7 -> 2; matrix products, arithmetic and copies ran while one was open for 11% -> 8% of each run, Pallas kernels for 0% -> 11%
where the time goes in v1:
time: 176 us; the launch traced here: 175 us
  blocking collectives  78.4 us (45%)
  local copies, waits for them, and re-layouts  38.6 us (22%)
  Pallas kernels  23.7 us (13%)
  waiting for transfers between devices  14.2 us (8%)
  between operations  14.2 us (8%)
  starting transfers between devices  3.62 us (2%)
  other arithmetic  1.83 us (1%)
    unnamed x42, local copies, waits for them, and re-layouts  31.9 us
    all_to_all x1, blocking collectives, on_device(): lax.all_to_all(sent.reshape(halves * slots, 2 * images, features), peers,...  25.7 us
    all_to_all x1, blocking collectives, on_device(): ret = lax.all_to_all(ret, peers, 0, 0, tiled=True)  24.7 us
    all_to_all x1, blocking collectives, on_device(): lax.all_to_all(jnp.broadcast_to(sums[None], (n_peers, *sums.shape)), peer...  14.6 us
    all_to_all x1, blocking collectives, on_device(): sums = jnp.sum(lax.all_to_all(sums, 'z', 0, 0, tiled=True), axis=0)  13.3 us
    all_gather x1, waiting for transfers between devices, on_device(): lax.all_gather(jnp.concatenate([w_in[0], second], axis=0), 'z', axis=0, t...  12.3 us
    pallas_call x1, Pallas kernels, back(): pl.pallas_call(back_kernel, grid=(images,), in_specs=[image, image, image...  10.4 us
    pallas_call x1, Pallas kernels, front(): pl.pallas_call(front_kernel, grid=(images,), in_specs=[image, image, pl.B...  8.27 us
  transfers between devices with their start and end apart: 3, of which 2 were waited for; matrix products, arithmetic and copies ran while one was open for 8% of the time, Pallas kernels for 11%

profile of v1, /device:TPU:1, one launch (start us, length us, event | category | flops | bytes accessed | tf_op | source)
XLA Modules:
  0.0 174.5 jit_solution(3177118367876566003)
XLA Ops:
  7.2 1.0 copy.46
  8.3 1.8 %pad_maximum_fusion = bf16[2048,128]{1,0:T(8,128)(2,1)} fusion(bf16[1024,128]{1,0:T(8,128)(2,1)S(1)} %bitcast.33, bf16[1024,128]{1,0:T(8,128)(2,1)} %bitcast.35), kind=kLoop, calls=%fused_computation | loop fusion | flops 1048576 | bytes 1048576 | tf_op jit(solution)/shard_map/concatenate | solution.py:295
  11.8 3.8 %copy.40.x_ref = bf16[8,196,1024]{2,1,0:T(8,128)(2,1)S(1)} copy(bf16[8,196,1024]{2,0,1:T(8,128)(2,1)} %param.6) | data formatting | bytes 6422528 | tf_op args[0]
  15.6 1.8 %copy.41.c_ref = bf16[8,196,1024]{2,1,0:T(8,128)(2,1)S(1)} copy(bf16[8,196,1024]{2,0,1:T(8,128)(2,1)S(1)} %copy-done.18) | data formatting | bytes 6422528 | tf_op args[5]
  17.4 8.3 %front.1 = (bf16[2,16,16,1024]{3,2,1,0:T(8,128)(2,1)S(1)}, bf16[8,196,1024]{2,1,0:T(8,128)(2,1)S(1)}, f32[8,196,128]{2,1,0:T(8,128)S(1)}, f32[8,196,128]{2,1,0:T...) custom-call(bf16[8,196,1024]{2,1,0:T(8,128)(2,1)S(1)} %copy.40.x_ref, ...), custom_call_target="tpu_custom_call" | custom-call | flops 4000000000 | bytes 14680064 | tf_op jit(solution)/shard_map/front/pallas_call | solution.py:71
  25.7 1.7 copy-done.9
  27.4 0.9 copy-done.10
  28.3 1.0 copy-done.12
  29.3 0.9 copy-done.14
  30.2 0.9 copy-done.16
  31.1 25.7 %all_to_all.25.act_ref = bf16[32,16,1024]{2,1,0:T(8,128)(2,1)} all-to-all(bf16[32,16,1024]{2,1,0:T(8,128)(2,1)S(1)} %bitcast.27), channel_id=1, replica_groups=mesh['yh'=2,'z'=8,'expert'=16] {'yh','expert'}, dimensions={0} | all-to-all | bytes 2097152 | tf_op jit(solution)/shard_map/all_to_all | solution.py:300
  56.8 12.3 %all-gather.3.cloned.1.call-done = bf16[16384,128]{1,0:T(8,128)(2,1)} async-done(((bf16[2048,128]{1,0:T(8,128)(2,1)}), bf16[16384,128]{1,0:T(8,128)(2,1)}) %all-gather.3.cloned.1.call-update) | async-done | bytes 4194320 | tf_op jit(solution)/shard_map/all_gather | solution.py:295
  69.0 1.2 copy-done.5
  70.2 2.2 %copy-done.7 = bf16[16384,128]{1,0:T(8,128)(2,1)S(1)} copy-done((bf16[16384,128]{1,0:T(8,128)(2,1)S(1)}, bf16[16384,128]{1,0:T(8,128)(2,1)}, u32[]{:S(2)}) %copy-start.7) | copy-done | bytes 4194328
  72.4 5.0 %expert.1 = (bf16[32,16,1024]{2,1,0:T(8,128)(2,1)S(1)}, bf16[8,2048,128]{2,1,0:T(8,128)(2,1)S(1)}) custom-call(bf16[32,16,1024]{2,1,0:T(8,128)(2,1)S(1)} %copy-done.5, bf16[8,2048,128]{2,1,0:T(8,128)(2,1)S(1)} %bitcast.28), custom_call_target="tpu_custom_call" | custom-call | flops 4000000000 | bytes 10485760 | tf_op jit(solution)/shard_map/expert/pallas_call | solution.py:166
  77.4 1.9 %copy-done = bf16[8,2048,128]{2,1,0:T(8,128)(2,1)} copy-done((bf16[8,2048,128]{2,1,0:T(8,128)(2,1)}, bf16[8,2048,128]{2,1,0:T(8,128)(2,1)S(1)}, u32[]{:S(2)}) %copy-start) | copy-done | bytes 4194328
  79.4 1.0 copy-done.4
  80.4 24.7 %all_to_all.26 = bf16[32,16,1024]{2,1,0:T(8,128)(2,1)S(1)} all-to-all(bf16[32,16,1024]{2,1,0:T(8,128)(2,1)} %copy-done.4), channel_id=1, replica_groups=mesh['yh'=2,'z'=8,'expert'=16] {'yh','expert'}, dimensions={0} | all-to-all | bytes 2097152 | tf_op jit(solution)/shard_map/all_to_all | solution.py:305
  105.1 2.0 %copy-done.2 = bf16[8,196,1024]{2,1,0:T(8,128)(2,1)S(1)} copy-done((bf16[8,196,1024]{2,1,0:T(8,128)(2,1)S(1)}, bf16[8,196,1024]{2,1,0:T(8,128)(2,1)}, u32[]{:S(2)}) %copy-start.2) | copy-done | bytes 3211288
  107.1 1.2 copy-done.11
  108.2 1.1 copy-done.13
  109.4 1.1 copy-done.15
  110.5 1.2 copy-done.17
  111.7 10.4 %back.1 = (bf16[8,196,1024]{2,1,0:T(8,128)(2,1)S(1)}, f32[8,24,128]{2,1,0:T(8,128)S(1)}) custom-call(bf16[8,196,1024]{2,1,0:T(8,128)(2,1)S(1)} %copy.40.x_ref, bf16[8,196,1024]{2,1,0:T(8,128)(2,1)S(1)} %copy-done.2, bf16[8,196,1024]{2,1,0:T(8,128)(2,1)} %copy-done.9, f32[8,196,128]{2,1,0:T(8,128)S(1)} %copy-done.11, f32[8,196,128]{2,1,0:T(8,128)S(1)} %copy-done.13, ...), custom_call_target="tpu_custom_call" | custom-call | flops 6000000000 | bytes 18874368 | tf_op jit(solution)/shard_map/back/pallas_call | solution.py:254
  122.1 1.7 copy-done.3
  123.8 13.3 %all_to_all.27 = f32[8,24,128]{2,1,0:T(8,128)S(1)} all-to-all(f32[8,24,128]{2,1,0:T(8,128)S(1)} %get-tuple-element.23), channel_id=1, replica_groups=mesh['yh'=2,'z'=8,'expert'=16] {'z'}, dimensions={0} | all-to-all | bytes 196608 | tf_op jit(solution)/shard_map/all_to_all | solution.py:310
  137.2 14.6 %all_to_all.28 = f32[32,24,128]{2,1,0:T(8,128)S(1)} all-to-all(f32[32,24,128]{2,1,0:T(8,128)S(1)} %broadcast_in_dim.10), channel_id=1, replica_groups=mesh['yh'=2,'z'=8,'expert'=16] {'yh','expert'}, dimensions={0} | all-to-all | bytes 786432 | tf_op jit(solution)/shard_map/all_to_all | solution.py:313
  152.5 3.5 %all-to-all-start.4 = ((f32[8,24,128]{2,1,0:T(8,128)}), f32[8,24,128]{2,1,0:T(8,128)S(1)}, u32[]{:S(2)}, u32[]{:S(2)}) async-start(f32[8,24,128]{2,1,0:T(8,128)} %broadcast_in_dim.22), calls=%async_computation.4 | async-start | bytes 196608 | tf_op jit(solution)/shard_map/all_to_all | solution.py:316
  156.1 5.4 %copy.44 = bf16[8,196,1024]{2,0,1:T(8,128)(2,1)} copy(bf16[8,196,1024]{2,1,0:T(8,128)(2,1)} %copy-done.3) | data formatting | bytes 6422528
  161.4 1.9 %all-to-all-done.4 = f32[8,24,128]{2,1,0:T(8,128)S(1)} async-done(((f32[8,24,128]{2,1,0:T(8,128)}), f32[8,24,128]{2,1,0:T(8,128)S(1)}, u32[]{:S(2)}, u32[]{:S(2)}) %all-to-all-start.4) | async-done | bytes 98336 | tf_op jit(solution)/shard_map/all_to_all | solution.py:316
  164.6 1.9 %fusion = (f32[1,1024,128]{2,1,0:T(8,128)S(1)}, f32[1,1024,128]{2,1,0:T(8,128)}) fusion(bf16[1,2048,128]{2,1,0:T(8,128)(2,1)} %reduce-scatter.2.cloned.1.call-done), kind=kLoop, calls=%fused_computation.5 | loop fusion | bytes 2097152 | tf_op jit(solution)/shard_map/slice | solution.py:320
  166.8 0.9 broadcast_in_dim_reshape.3
  (38 shorter events, 4.1 us)
Async XLA Ops:
  7.2 61.9 %all-gather.3.cloned.1.call-start = ((), (), s32[]{:S(2)}) async-start(), calls=%async_computation.7 | async-start | bytes 4718592 | tf_op jit(solution)/shard_map/all_gather | solution.py:295
  10.1 154.6 %reduce-scatter.2.cloned.1.call-start = ((), (), s32[]{:S(2)}) async-start(), calls=%async_computation.6 | async-start | bytes 4718592 | tf_op jit(solution)/shard_map/reduce_scatter | solution.py:304
  11.8 3.8 %copy-start.18 = (bf16[8,196,1024]{2,0,1:T(8,128)(2,1)S(1)}, bf16[8,196,1024]{2,0,1:T(8,128)(2,1)}, u32[]{:S(2)}) copy-start(bf16[8,196,1024]{2,0,1:T(8,128)(2,1)} %param.11) | copy-start | bytes 9633796
  15.6 1.8 %copy-start.6 = (bf16[1024,128]{1,0:T(8,128)(2,1)S(1)}, bf16[1024,128]{1,0:T(8,128)(2,1)}, u32[]{:S(2)}) copy-start(bf16[1024,128]{1,0:T(8,128)(2,1)} %copy.38.wrep_ref) | copy-start | bytes 786436
  15.6 1.8 %copy-start.8 = (f32[1024]{0:T(1024)S(1)}, f32[1024]{0:T(1024)}, u32[]{:S(2)}) copy-start(f32[1024]{0:T(1024)} %param.7) | copy-start | bytes 12292
  17.4 8.3 %copy-start.1 = (bf16[8,196,1024]{2,1,0:T(8,128)(2,1)}, bf16[8,196,1024]{2,1,0:T(8,128)(2,1)S(1)}, u32[]{:S(2)}) copy-start(bf16[8,196,1024]{2,1,0:T(8,128)(2,1)S(1)} %copy.41.c_ref) | copy-start | bytes 9633796
  25.7 1.7 copy-start.9
  27.4 0.9 copy-start.10
  28.3 1.0 copy-start.12
  29.3 0.9 copy-start.14
  30.2 0.9 copy-start.16
  69.0 1.2 copy-start.5
  70.2 2.2 %copy-start.7 = (bf16[16384,128]{1,0:T(8,128)(2,1)S(1)}, bf16[16384,128]{1,0:T(8,128)(2,1)}, u32[]{:S(2)}) copy-start(bf16[16384,128]{1,0:T(8,128)(2,1)} %all-gather.3.cloned.1.call-done) | copy-start | bytes 12582916
  77.4 1.9 %copy-start = (bf16[8,2048,128]{2,1,0:T(8,128)(2,1)}, bf16[8,2048,128]{2,1,0:T(8,128)(2,1)S(1)}, u32[]{:S(2)}) copy-start(bf16[8,2048,128]{2,1,0:T(8,128)(2,1)S(1)} %get-tuple-element.24) | copy-start | bytes 12582916
  79.4 1.0 copy-start.4
  105.1 2.0 %copy-start.2 = (bf16[8,196,1024]{2,1,0:T(8,128)(2,1)S(1)}, bf16[8,196,1024]{2,1,0:T(8,128)(2,1)}, u32[]{:S(2)}) copy-start(bf16[8,196,1024]{2,1,0:T(8,128)(2,1)} %copy-done.1) | copy-start | bytes 9633796
  107.1 1.2 copy-start.11
  108.2 1.1 copy-start.13
  109.4 1.1 copy-start.15
  110.5 1.2 copy-start.17
  122.1 1.7 copy-start.3
  152.5 10.9 %all-to-all-start.4 = ((f32[8,24,128]{2,1,0:T(8,128)}), f32[8,24,128]{2,1,0:T(8,128)S(1)}, u32[]{:S(2)}, u32[]{:S(2)}) async-start(f32[8,24,128]{2,1,0:T(8,128)} %broadcast_in_dim.22), calls=%async_computation.4 | async-start | bytes 196608 | tf_op jit(solution)/shard_map/all_to_all | solution.py:316
Sparse Core Ops, SparseCore 0:
  10.4 58.6 all-gather.2
  80.5 55.5 reduce-scatter.1

commit v2 on v0

v2 whole, which is shorter than its diff:
```python
import functools

import jax
import jax.numpy as jnp
from jax import lax
from jax.experimental import pallas as pl
from jax.experimental.pallas import tpu as pltpu
from jax.sharding import Mesh
from jax.sharding import PartitionSpec as P

eps = 1e-06
f32 = jnp.float32
bf16 = jnp.bfloat16
VMEM = 60 * 1024 * 1024
RING = 3 * 10**9
RING2 = 3 * 10**9


def dot(a, b, ca, cb):
    return lax.dot_general(a, b, (((ca,), (cb,)), ((), ())), preferred_element_type=f32)


def own(shape, images):
    row = lax.broadcasted_iota(jnp.int32, shape, 0)
    col = lax.broadcasted_iota(jnp.int32, shape, 1)
    return lax.rem(row, images) == lax.rem(col, images)


def replicated(slot_ref, images):
    slots, features = slot_ref.shape
    rows = jnp.broadcast_to(slot_ref[...].astype(f32)[:, None, :], (slots, images, features))
    return rows.reshape(slots * images, features).astype(bf16)


def cuts(rows, shares):
    groups = rows // 16
    at = 0
    out = []
    for k, share in enumerate(shares):
        size = groups - at if k == len(shares) - 1 else groups * share // sum(shares)
        if size:
            out.append(pl.ds(at * 16, size * 16 if k < len(shares) - 1 else rows - at * 16))
        at += size
    return out


def copies_of(src, dst, sem, slices):
    return [pltpu.make_async_copy(src.at[r], dst.at[r], sem.at[k]) for k, r in enumerate(slices)]


def row_softmax(logits, images):
    mine = own(logits.shape, images)
    ec = jnp.where(mine, jnp.exp(logits - jnp.max(logits, axis=1, keepdims=True)), 0.0)
    return ec / jnp.sum(ec, axis=1, keepdims=True)


def front_kernel(
    shares, gain_ref, slot_ref, x_ref, c_ref, out_ref, normed_ref, acc_ref, col_ref,
    x_s, c_s, out_s, normed_s, lg_s, acc_s, x_sem, c_sem, normed_sem, last_sem,
):
    slots, features = slot_ref.shape
    copies, _, images, _ = out_s.shape
    images = images // 2
    slices = cuts(x_s.shape[0], shares)
    x_in = copies_of(x_ref, x_s, x_sem, slices)
    c_in = copies_of(c_ref, c_s, c_sem, slices)
    normed_out = copies_of(normed_s, normed_ref, normed_sem, slices)
    for one, two in zip(x_in, c_in):
        one.start()
        two.start()
    wrep = replicated(slot_ref, images)
    gain = gain_ref[...]
    cot_slots = 0.0
    for k, r in enumerate(slices):
        x_in[k].wait()
        x = x_s[r].astype(f32)
        xc = x - jnp.mean(x, axis=-1, keepdims=True)
        inv = lax.rsqrt(jnp.mean(xc * xc, axis=-1, keepdims=True) + eps)
        normed = (xc * inv * gain).astype(bf16)
        normed_s[r] = normed
        normed_out[k].start()
        logits = dot(normed, wrep, 1, 1)
        lg_s[r] = logits
        pc = row_softmax(logits, images)
        c_in[k].wait()
        cot_slots = cot_slots + dot(pc.astype(bf16), c_s[r], 0, 0)
    lg = lg_s[...]
    lg = jnp.where(own(lg.shape, images), lg, -jnp.inf)
    most = jnp.max(lg, axis=0, keepdims=True)
    ed = jnp.exp(lg - most)
    total = jnp.sum(ed, axis=0, keepdims=True)
    pd = ed / total
    row = lax.broadcasted_iota(jnp.int32, col_ref.shape, 0)
    col_ref[...] = jnp.where(row == 0, most, total)
    got = dot(pd.astype(bf16), normed_s[...], 0, 0)
    both = [got.reshape(slots, images, features), cot_slots.reshape(slots, images, features)]
    both = jnp.concatenate(both, axis=1).astype(bf16)
    for copy in range(copies):
        out_s[copy] = both
    acc_s[...] = got
    last = [
        pltpu.make_async_copy(src, dst, last_sem.at[j])
        for j, (src, dst) in enumerate(((out_s, out_ref), (acc_s, acc_ref)))
    ]
    for copy in last:
        copy.start()
    for copy in normed_out + last:
        copy.wait()


vmem = pl.BlockSpec(memory_space=pltpu.VMEM)
anywhere = pl.BlockSpec(memory_space=pl.ANY)


def front(tokens, norm_gain, slot_t, cotangent, images, copies, shares=(1, 1)):
    rows, features = tokens.shape
    slots = slot_t.shape[0]
    wide = slots * images
    n = len(shares)
    sent = ((copies, slots, 2 * images, features), bf16)
    acc = ((wide, features), f32)
    return pl.pallas_call(
        functools.partial(front_kernel, shares),
        in_specs=[vmem, vmem, anywhere, anywhere],
        out_specs=[anywhere] * 3 + [vmem],
        out_shape=[
            jax.ShapeDtypeStruct(*sent),
            jax.ShapeDtypeStruct((rows, features), bf16),
            jax.ShapeDtypeStruct(*acc),
            jax.ShapeDtypeStruct((8, wide), f32),
        ],
        scratch_shapes=[pltpu.VMEM(tokens.shape, bf16)] * 2
        + [
            pltpu.VMEM(*sent),
            pltpu.VMEM(tokens.shape, bf16),
            pltpu.VMEM((rows, wide), f32),
            pltpu.VMEM(*acc),
            pltpu.SemaphoreType.DMA((n,)),
            pltpu.SemaphoreType.DMA((n,)),
            pltpu.SemaphoreType.DMA((n,)),
            pltpu.SemaphoreType.DMA((2,)),
        ],
        compiler_params=pltpu.CompilerParams(vmem_limit_bytes=VMEM),
        cost_estimate=pl.CostEstimate(flops=8 * 10**9, bytes_accessed=14 * 2**20, transcendentals=10**6),
        name="front",
    )(norm_gain, slot_t, tokens, cotangent)


gelu_c = 0.7978845608028654
gelu_k = 0.044715


def expert_kernel(at_ref, act_ref, *refs):
    n = (len(refs) - 14) // 2
    firsts, seconds = refs[:n], refs[n : 2 * n]
    (
        ret_ref, dw_ref, act_s, w1_s, w2_s, dw_s, ret_s, y_acc, g_acc, act_sem, w1_sem, w2_sem, dw_sem, ret_sem,
    ) = refs[2 * n :]
    peers, rows, features = act_s.shape
    half = rows // 2
    part = seconds[0].shape[0]
    groups = w1_s.shape[0]
    size = n // groups
    act_copy = pltpu.make_async_copy(act_ref, act_s, act_sem)
    act_copy.start()
    copies = []
    for r in range(n):
        g, q = r // size, r % size
        one = pltpu.make_async_copy(firsts[r], w1_s.at[g, :, pl.ds(q * part, part)], w1_sem.at[r])
        two = pltpu.make_async_copy(seconds[r], w2_s.at[g, pl.ds(q * part, part)], w2_sem.at[r])
        one.start()
        two.start()
        copies.append((one, two))
    act_copy.wait()
    act = act_s[...].astype(f32)
    slots = act[:, :half].reshape(peers * half, features).astype(bf16)
    cots = act[:, half:].reshape(peers * half, features).astype(bf16)
    sends = []
    for g in range(groups):
        for q in range(size):
            copies[g * size + q][0].wait()
            copies[g * size + q][1].wait()
        w1 = w1_s[g]
        w2 = w2_s[g]
        pre = dot(slots, w1, 1, 0)
        sq = pre * pre
        th = jnp.tanh(gelu_c * (pre + gelu_k * (sq * pre)))
        cdf = 0.5 * (1.0 + th)
        hidden = (pre * cdf).astype(bf16)
        slope = cdf + 0.5 * pre * (1.0 - th * th) * (gelu_c * (1.0 + 3.0 * gelu_k * sq))
        d_act = (dot(cots, w2, 1, 1) * slope).astype(bf16)
        y = dot(hidden, w2, 1, 0)
        grad = dot(d_act, w1, 1, 1)
        if g:
            y = y + y_acc[...]
            grad = grad + g_acc[...]
        if g < groups - 1:
            y_acc[...] = y
            g_acc[...] = grad
        else:
            ret_s[...] = jnp.concatenate(
                [y.reshape(peers, half, features), grad.reshape(peers, half, features)], axis=1
            ).astype(bf16)
            ret_copy = pltpu.make_async_copy(ret_s, ret_ref, ret_sem)
            ret_copy.start()
        d_w1 = dot(slots, d_act, 0, 0).astype(bf16)
        d_w2 = dot(hidden, cots, 0, 0).astype(bf16)
        for q in range(size):
            r = g * size + q
            mine = slice(q * part, (q + 1) * part)
            dw_s[r, :features] = d_w1[:, mine]
            for j in range(features // part):
                dw_s[r, pl.ds(features + j * part, part)] = d_w2[mine, j * part : (j + 1) * part]
            send = pltpu.make_async_copy(dw_s.at[r], dw_ref.at[lax.rem(at_ref[0] + r, n)], dw_sem.at[r])
            send.start()
            sends.append(send)
    ret_copy.wait()
    for send in sends:
        send.wait()


def expert(at, act, firsts, seconds):
    peers, rows, features = act.shape
    part = firsts[0].shape[1]
    n = len(firsts)
    all_rows = peers * rows // 2
    size = 2
    return pl.pallas_call(
        expert_kernel,
        in_specs=[pl.BlockSpec(memory_space=pltpu.SMEM)] + [anywhere] * (1 + 2 * n),
        out_specs=[anywhere, anywhere],
        out_shape=[
            jax.ShapeDtypeStruct((peers, rows, features), bf16),
            jax.ShapeDtypeStruct((n, 2 * features, part), bf16),
        ],
        scratch_shapes=[
            pltpu.VMEM((peers, rows, features), bf16),
            pltpu.VMEM((n // size, features, size * part), bf16),
            pltpu.VMEM((n // size, size * part, features), bf16),
            pltpu.VMEM((n, 2 * features, part), bf16),
            pltpu.VMEM((peers, rows, features), bf16),
            pltpu.VMEM((all_rows, features), f32),
            pltpu.VMEM((all_rows, features), f32),
            pltpu.SemaphoreType.DMA,
            pltpu.SemaphoreType.DMA((n,)),
            pltpu.SemaphoreType.DMA((n,)),
            pltpu.SemaphoreType.DMA((n,)),
            pltpu.SemaphoreType.DMA,
        ],
        compiler_params=pltpu.CompilerParams(vmem_limit_bytes=VMEM),
        cost_estimate=pl.CostEstimate(flops=4 * 10**9, bytes_accessed=10 * 2**20, transcendentals=10**6),
        name="expert",
    )(at, act, *firsts, *seconds)


def route_kernel(
    shares, gain_ref, slot_ref, col_ref, c_ref, normed_ref, ret_ref, acc_ref,
    sums_ref, coef_ref, grad_ref,
    c_s, normed_s, ret_s, acc_s, coef_s, grad_s, out_s, pd_s, dd_s, fc_s,
    c_sem, normed_sem, whole_sem, coef_sem,
):
    copies, slots, images, features = ret_s.shape
    images = images // 2
    wide = slots * images
    slices = cuts(c_s.shape[0], shares)
    c_in = copies_of(c_ref, c_s, c_sem, slices)
    normed_in = copies_of(normed_ref, normed_s, normed_sem, slices)
    coef_out = copies_of(coef_s, coef_ref, coef_sem, slices)
    ret_in = pltpu.make_async_copy(ret_ref, ret_s, whole_sem.at[0])
    acc_in = pltpu.make_async_copy(acc_ref, acc_s, whole_sem.at[1])
    grad_out = pltpu.make_async_copy(grad_s, grad_ref, whole_sem.at[2])
    normed_in[0].start()
    ret_in.start()
    c_in[0].start()
    for k in range(1, len(slices)):
        normed_in[k].start()
        c_in[k].start()
    acc_in.start()
    wrep = replicated(slot_ref, images)
    grad_s[wide:] = wrep
    most, total = col_ref[0:1], col_ref[1:2]
    ret_in.wait()
    got = ret_s[0].astype(f32)
    for copy in range(1, copies):
        got = got + ret_s[copy].astype(f32)
    out_s[...] = got[:, :images].reshape(wide, features).astype(bf16)
    grad_s[:wide] = got[:, images:].reshape(wide, features).astype(bf16)
    grad_out.start()
    col_sum = jnp.zeros((1, wide), f32)
    for k, r in enumerate(slices):
        normed_in[k].wait()
        logits = dot(normed_s[r], wrep, 1, 1)
        pc = row_softmax(logits, images)
        pd = jnp.where(own(logits.shape, images), jnp.exp(logits - most) / total, 0.0)
        dd = dot(normed_s[r], grad_s[:wide], 1, 1)
        c_in[k].wait()
        d_combine = dot(c_s[r], out_s[...], 1, 1)
        fc_s[r] = pc * (d_combine - jnp.sum(pc * d_combine, axis=1, keepdims=True))
        pd_s[r] = pd
        dd_s[r] = dd
        col_sum = col_sum + jnp.sum(pd * dd, axis=0, keepdims=True)
    for k, r in enumerate(slices):
        pd = pd_s[r]
        coef_s[r, :wide] = pd.astype(bf16)
        coef_s[r, wide:] = (fc_s[r] + pd * (dd_s[r] - col_sum)).astype(bf16)
        coef_out[k].start()
    acc = dot(coef_s[:, wide:], normed_s[...], 0, 0)
    acc_in.wait()
    d_weight = jnp.sum(acc.reshape(slots, images, features), axis=1)
    d_gain = jnp.sum(acc_s[...] * grad_s[:wide].astype(f32), axis=0, keepdims=True)
    d_gain = d_gain + jnp.sum(acc * grad_s[wide:].astype(f32), axis=0, keepdims=True)
    d_gain = d_gain / gain_ref[...]
    pieces, _, part = sums_ref.shape
    blocks = features // part // pieces
    for k in range(pieces):
        start = k * blocks * part
        for j in range(blocks):
            sums_ref[k, j * slots : (j + 1) * slots] = d_weight[:, start + j * part : start + (j + 1) * part]
        last = [d_gain[:, start + j * part : start + (j + 1) * part] for j in range(blocks)]
        last.append(jnp.zeros((8 - blocks, part), f32))
        sums_ref[k, blocks * slots :] = jnp.concatenate(last, axis=0)
    for copy in coef_out:
        copy.wait()
    grad_out.wait()


def route(cotangent, normed, norm_gain, slot_t, col, ret, acc, pieces, shares=(1, 1)):
    rows, features = cotangent.shape
    _, slots, images, _ = ret.shape
    wide = slots * images // 2
    n = len(shares)
    ins = (cotangent, normed, ret, acc)
    outs = [((rows, 2 * wide), bf16), ((2 * wide, features), bf16)]
    sums = jax.ShapeDtypeStruct((pieces, features // 128 // pieces * slots + 8, 128), f32)
    return pl.pallas_call(
        functools.partial(route_kernel, shares),
        in_specs=[vmem] * 3 + [anywhere] * len(ins),
        out_specs=[vmem] + [anywhere] * len(outs),
        out_shape=[sums] + [jax.ShapeDtypeStruct(*out) for out in outs],
        scratch_shapes=[pltpu.VMEM(x.shape, x.dtype) for x in ins]
        + [pltpu.VMEM(*out) for out in outs]
        + [
            pltpu.VMEM((wide, features), bf16),
            pltpu.VMEM((rows, wide), f32),
            pltpu.VMEM((rows, wide), f32),
            pltpu.VMEM((rows, wide), f32),
            pltpu.SemaphoreType.DMA((n,)),
            pltpu.SemaphoreType.DMA((n,)),
            pltpu.SemaphoreType.DMA((3,)),
            pltpu.SemaphoreType.DMA((n,)),
        ],
        compiler_params=pltpu.CompilerParams(vmem_limit_bytes=VMEM),
        cost_estimate=pl.CostEstimate(flops=5 * 10**9, bytes_accessed=14 * 2**20, transcendentals=0),
        name="route",
    )(norm_gain, slot_t, col, *ins)


def back_kernel(gain_ref, grad_ref, x_ref, coef_ref, dt_ref):
    x = x_ref[...].astype(f32)
    xc = x - jnp.mean(x, axis=-1, keepdims=True)
    inv = lax.rsqrt(jnp.mean(xc * xc, axis=-1, keepdims=True) + eps)
    x_hat = xc * inv
    scaled = dot(coef_ref[...], grad_ref[...], 1, 0) * gain_ref[...]
    mean_scaled = jnp.mean(scaled, axis=-1, keepdims=True)
    mean_dot = jnp.mean(scaled * x_hat, axis=-1, keepdims=True)
    dt_ref[...] = (inv * (scaled - mean_scaled - x_hat * mean_dot)).astype(bf16)


def back(tokens, coef, norm_gain, grad):
    rows, features = tokens.shape
    wide = coef.shape[1]
    steps = 2 if rows % 32 == 0 else 1
    block = pl.BlockSpec((rows // steps, features), lambda i: (i, 0))
    return pl.pallas_call(
        back_kernel,
        grid=(steps,),
        in_specs=[
            pl.BlockSpec((1, features), lambda i: (0, 0)),
            pl.BlockSpec((wide, features), lambda i: (0, 0)),
            block,
            pl.BlockSpec((rows // steps, wide), lambda i: (i, 0)),
        ],
        out_specs=block,
        out_shape=jax.ShapeDtypeStruct(tokens.shape, bf16),
        compiler_params=pltpu.CompilerParams(vmem_limit_bytes=VMEM),
        cost_estimate=pl.CostEstimate(flops=5 * 10**9, bytes_accessed=8 * 2**20, transcendentals=0),
        name="back",
    )(norm_gain, grad, tokens, coef)


def gate_kernel(*refs):
    pass


def after(kept, others, weight=0):
    return pl.pallas_call(
        gate_kernel,
        in_specs=[anywhere] * (len(kept) + len(others)),
        out_specs=[anywhere] * len(kept),
        out_shape=[jax.ShapeDtypeStruct(x.shape, x.dtype) for x in kept],
        input_output_aliases={i: i for i in range(len(kept))},
        cost_estimate=pl.CostEstimate(flops=weight, bytes_accessed=0, transcendentals=0),
        name="after",
    )(*kept, *others)


def on_device(tokens, norm_gain, slot_weight, w_in, w_out, cotangent):
    images, _, features = tokens.shape
    slots = slot_weight.shape[1]
    part = w_in.shape[2]
    halves = lax.axis_size("yh")
    peers = ("yh", "yl", "x", "c")

    n = lax.axis_size("z")
    up = [(i, (i + 1) % n) for i in range(n)]
    down = [(i, (i - 1) % n) for i in range(n)]
    firsts = {0: w_in[0]}
    seconds = {0: w_out[0]}

    def step(k):
        firsts[n - k] = lax.ppermute(firsts[(n - k + 1) % n], "z", up)
        seconds[k] = lax.ppermute(seconds[k - 1], "z", down)
        if k < n - k:
            firsts[k] = lax.ppermute(firsts[k - 1], "z", down)
            seconds[n - k] = lax.ppermute(seconds[(n - k + 1) % n], "z", up)

    step(1)
    gain = norm_gain[None]
    slot_t = slot_weight.T
    tok = tokens.shape[1]
    by_place = tokens.swapaxes(0, 1).reshape(tok * images, features)
    cots = cotangent.swapaxes(0, 1).reshape(tok * images, features)
    sent, normed, acc, col = front(by_place, gain, slot_t, cots, images, halves)
    sent, firsts[1], firsts[n - 1], seconds[1], seconds[n - 1] = after(
        [sent, firsts[1], firsts[n - 1], seconds[1], seconds[n - 1]], []
    )
    act = lax.all_to_all(
        sent.reshape(halves * slots, 2 * images, features), peers, 0, 0, tiled=True
    )
    for k in range(2, n // 2 + 1):
        step(k)
    far = n // 2
    firsts[far], seconds[far] = after([firsts[far], seconds[far]], [], RING)
    if n > 3:
        firsts[far - 1], seconds[far + 1] = after([firsts[far - 1], seconds[far + 1]], [], RING2)
    at = lax.axis_index("z").reshape(1)
    ret, d_w = expert(at, act, [firsts[r] for r in range(n)], [seconds[r] for r in range(n)])
    d_w = lax.psum_scatter(d_w, "z", scatter_dimension=0, tiled=False).astype(f32)
    ret = lax.all_to_all(ret, peers, 0, 0, tiled=True)
    cores = lax.axis_size("c")
    ret = ret.reshape(halves, slots, 2 * images, features)
    sums, coef, grad = route(cots, normed, gain, slot_t, col, ret, acc, cores)

    core = lax.axis_index("c")
    swap = [(0, 1), (1, 0)]
    other = lax.ppermute(lax.dynamic_index_in_dim(sums, 1 - core, 0, False), "c", swap)
    share = lax.dynamic_index_in_dim(sums, core, 0, False) + other

    def total(share, axes, others=()):
        many = 1
        for axis in axes:
            many *= lax.axis_size(axis)
        copies = jnp.broadcast_to(share[None], (many, *share.shape))
        (copies,) = after([lax.all_to_all(copies, axes, 0, 0, tiled=True)], others)
        return jnp.sum(copies, axis=0)

    d_tokens = back(by_place, coef, gain, grad)
    share = total(share, ("yh", "yl", "x"), [d_tokens])
    pieces = features // part
    d_first = d_w[:features]
    d_second = d_w[features:].reshape(pieces, part, part).swapaxes(0, 1).reshape(part, features)
    share = total(share, ("z",), [d_first, d_second])
    other = lax.ppermute(share, "c", swap)
    sums = jnp.stack([jnp.where(core == 0, share, other), jnp.where(core == 0, other, share)])
    blocks = features // sums.shape[2] // cores
    d_slot_weight = sums[:, : blocks * slots].reshape(cores * blocks, slots, -1)
    d_slot_weight = d_slot_weight.swapaxes(0, 1).reshape(slots, features).T
    d_gain = sums[:, blocks * slots : blocks * slots + blocks].reshape(features)
    d_tokens = d_tokens.reshape(tok, images, features).swapaxes(0, 1)
    return (d_tokens, d_slot_weight, d_gain, d_first[None], d_second[None])


def solution(mesh):
    fine = Mesh(
        mesh.devices.reshape(2, mesh.shape["dp"] // 2, 2, mesh.shape["expert"] // 4, 2),
        ("yh", "z", "yl", "x", "c"),
    )
    everywhere = P(("yh", "z", "yl", "x", "c"), None, None)
    first = P(("yl", "x", "c"), None, ("yh", "z"))
    second = P(("yl", "x", "c"), ("yh", "z"), None)
    return jax.shard_map(
        on_device,
        mesh=fine,
        in_specs=(everywhere, P(), P(), first, second, everywhere),
        out_specs=(everywhere, P(), P(), first, second),
        check_vma=False,
    )
```

time: 912 us -> 158 us (0.17)
  waiting for transfers between devices: 675 us -> 45.3 us
  blocking collectives: 74.6 us -> 0 us
  matrix products: 73 us -> 0 us
  Pallas kernels: 0 us -> 32.7 us
  starting transfers between devices: 26.1 us -> 48.9 us
  other arithmetic: 23.1 us -> 3.47 us
    psum x1 -> x0, waiting for transfers between devices: 245 us -> none  [on_device(): d_slot_weight, d_gain = lax.psum((weight_part, gain_part), ('dp', 'expert'))]
    reduce_scatter x1, waiting for transfers between devices: 209 us -> 0.02 us  [on_device(): lax.psum_scatter(d_w, 'z', scatter_dimension=0, tiled=False).astype(f32)]
    all_gather x2 -> x0, waiting for transfers between devices: 158 us -> none  [the longest x1 95.4 us: on_device(): second_layer = lax.all_gather(second_part, 'dp', axis=0, tiled=True)]
    psum x1 -> x0, blocking collectives: 74.6 us -> none  [on_device(): d_slot_weight, d_gain = lax.psum((weight_part, gain_part), ('dp', 'expert'))]
    dot_general x14 -> x0, matrix products: 73 us -> none  [the longest x1 12.3 us: on_device(): jnp.einsum('bts,sbd->btd', dispatch, grad_slots, preferred_element_type=j...]
    unnamed x6 -> x1, waiting for transfers between devices: 58.2 us -> 0.02 us
    pallas_call x0 -> x9, Pallas kernels: none -> 32.7 us  [the longest x1 8.76 us: front(): pl.pallas_call(functools.partial(front_kernel, shares), in_specs=[vmem, v...]
    all_to_all x4, waiting for transfers between devices: 5.17 us -> 29.4 us  [the longest x1 17.2 us: on_device(): ret = lax.all_to_all(ret, peers, 0, 0, tiled=True)]
  transfers between devices with their start and end apart: 9 -> 21, of which waited for: 7 -> 9; matrix products, arithmetic and copies ran while one was open for 11% -> 5% of each run, Pallas kernels for 0% -> 15%
where the time goes in v2:
time: 158 us; the launch traced here: 157 us
  starting transfers between devices  48.9 us (31%)
  waiting for transfers between devices  45.3 us (29%)
  Pallas kernels  32.7 us (21%)
  between operations  14.3 us (9%)
  local copies, waits for them, and re-layouts  12.7 us (8%)
  other arithmetic  3.47 us (2%)
    all_to_all x1, waiting for transfers between devices, on_device(): ret = lax.all_to_all(ret, peers, 0, 0, tiled=True)  17.2 us
    all_to_all x2, waiting for transfers between devices, total(): copies, = after([lax.all_to_all(copies, axes, 0, 0, tiled=True)], others)  12.3 us
    ppermute x4, starting transfers between devices, step(): seconds[k] = lax.ppermute(seconds[k - 1], 'z', down)  10.7 us
    all_to_all x1, starting transfers between devices, on_device(): lax.all_to_all(sent.reshape(halves * slots, 2 * images, features), peers,...  10.1 us
    ppermute x4, waiting for transfers between devices, step(): firsts[n - k] = lax.ppermute(firsts[(n - k + 1) % n], 'z', up)  9.6 us
    pallas_call x1, Pallas kernels, front(): pl.pallas_call(functools.partial(front_kernel, shares), in_specs=[vmem, v...  8.76 us
    pallas_call x1, Pallas kernels, route(): pl.pallas_call(functools.partial(route_kernel, shares), in_specs=[vmem] *...  8.74 us
    pallas_call x1, Pallas kernels, expert(): pl.pallas_call(expert_kernel, in_specs=[pl.BlockSpec(memory_space=pltpu.S...  8.39 us
  transfers between devices with their start and end apart: 21, of which 9 were waited for; matrix products, arithmetic and copies ran while one was open for 5% of the time, Pallas kernels for 15%

profile of v2, /device:TPU:1, one launch (start us, length us, event | category | flops | bytes accessed | tf_op | source)
XLA Modules:
  0.0 157.2 jit_solution(329760534561568999)
XLA Ops:
  7.2 6.5 %collective-permute-start = (bf16[1024,128]{1,0:T(8,128)(2,1)}, bf16[1024,128]{1,0:T(8,128)(2,1)S(1)}, u32[]{:S(2)}, u32[]{:S(2)}) collective-permute-start(bf16[1024,128]{1,0:T(8,128)(2,1)} %bitcast.59), channel_id=1, source_target_pairs={{0,112},{16,0},{32,16},{48,32},{64,48},{80,64},{96,80},{112,96},{1... | collective-permute-start | bytes 786440 | tf_op jit(solution)/shard_map/ppermute | solution.py:424
  13.7 2.7 %collective-permute-start.2 = (bf16[128,1024]{1,0:T(8,128)(2,1)}, bf16[128,1024]{1,0:T(8,128)(2,1)S(1)}, u32[]{:S(2)}, u32[]{:S(2)}) collective-permute-start(bf16[128,1024]{1,0:T(8,128)(2,1)} %bitcast.62), channel_id=1, source_target_pairs={{0,112},{16,0},{32,16},{48,32},{64,48},{80,64},{96,80},{112,96},{1... | collective-permute-start | bytes 786440 | tf_op jit(solution)/shard_map/ppermute | solution.py:422
  16.3 8.8 %front.1 = (bf16[2,16,16,1024]{3,2,1,0:T(8,128)(2,1)}, bf16[1568,1024]{1,0:T(8,128)(2,1)}, f32[128,1024]{1,0:T(8,128)}, f32[8,128]{1,0:T(8,128)}) custom-call(f32[1,1024]{1,0:T(1,128)} %bitcast.67, bf16[16,1024]{1,0:T(8,128)(2,1)} %bitcast.65, bf16[1568,1024]{1,0:T(8,128)(2,1)} %bitcast.57, bf16[1568,1024]{1,0:T(8,128)(2,1)} %bitcast.55), custom_call_target="tpu_custom_call" | custom-call | flops 8000000000 | bytes 14680064 | tf_op jit(solution)/shard_map/front/pallas_call | solution.py:122
  25.2 2.4 %collective-permute-done.3.refs_4_ = bf16[128,1024]{1,0:T(8,128)(2,1)S(1)} collective-permute-done((bf16[128,1024]{1,0:T(8,128)(2,1)}, bf16[128,1024]{1,0:T(8,128)(2,1)S(1)}, u32[]{:S(2)}, u32[]{:S(2)}) %collective-permute-start.3) | collective-permute-done | bytes 262176 | tf_op jit(solution)/shard_map/ppermute | solution.py:425
  28.3 2.7 %collective-permute-start.11 = (bf16[128,1024]{1,0:T(8,128)(2,1)}, bf16[128,1024]{1,0:T(8,128)(2,1)S(1)}, u32[]{:S(2)}, u32[]{:S(2)}) collective-permute-start(bf16[128,1024]{1,0:T(8,128)(2,1)} %get-tuple-element.31.refs_9_), channel_id=1, source_target_pairs={{0,112},{16,0},{32,16},{48,32},{64,48},{80,64},{96,80},{112,96},{1... | collective-permute-start | bytes 786440 | tf_op jit(solution)/shard_map/ppermute | solution.py:422
  31.0 1.4 collective-permute-start.6
  32.4 10.1 %all-to-all-start = ((bf16[32,16,1024]{2,1,0:T(8,128)(2,1)}), bf16[32,16,1024]{2,1,0:T(8,128)(2,1)S(1)}, u32[]{:S(2)}, u32[]{:S(2)}) async-start(bf16[32,16,1024]{2,1,0:T(8,128)(2,1)} %bitcast.46), calls=%async_computation | async-start | bytes 2097152 | tf_op jit(solution)/shard_map/all_to_all | solution.py:437
  42.7 2.6 %collective-permute-start.12 = (bf16[128,1024]{1,0:T(8,128)(2,1)S(1)}, bf16[128,1024]{1,0:T(8,128)(2,1)S(1)}, u32[]{:S(2)}, u32[]{:S(2)}) collective-permute-start(bf16[128,1024]{1,0:T(8,128)(2,1)S(1)} %collective-permute-done.11.refs_10_), channel_id=1, source_target_pairs={{0,112},{16,0},{32,16},{48,32},{64,48},{80,64},{96,80},{112,96},{1... | collective-permute-start | bytes 786440 | tf_op jit(solution)/shard_map/ppermute | solution.py:422
  45.4 1.4 collective-permute-start.7
  46.8 4.7 %collective-permute-done.9.refs_5_ = bf16[1024,128]{1,0:T(8,128)(2,1)S(1)} collective-permute-done((bf16[1024,128]{1,0:T(8,128)(2,1)S(1)}, bf16[1024,128]{1,0:T(8,128)(2,1)S(1)}, u32[]{:S(2)}, u32[]{:S(2)}) %collective-permute-start.9) | collective-permute-done | bytes 262176 | tf_op jit(solution)/shard_map/ppermute | solution.py:421
  51.5 2.7 %collective-permute-start.13 = (bf16[128,1024]{1,0:T(8,128)(2,1)S(1)}, bf16[128,1024]{1,0:T(8,128)(2,1)}, u32[]{:S(2)}, u32[]{:S(2)}) collective-permute-start(bf16[128,1024]{1,0:T(8,128)(2,1)S(1)} %collective-permute-done.12.refs_11_), channel_id=1, source_target_pairs={{0,112},{16,0},{32,16},{48,32},{64,48},{80,64},{96,80},{112,96},{1... | collective-permute-start | bytes 786440 | tf_op jit(solution)/shard_map/ppermute | solution.py:422
  54.2 2.0 %collective-permute-done.5.refs_0_ = bf16[1024,128]{1,0:T(8,128)(2,1)S(1)} collective-permute-done((bf16[1024,128]{1,0:T(8,128)(2,1)S(1)}, bf16[1024,128]{1,0:T(8,128)(2,1)S(1)}, u32[]{:S(2)}, u32[]{:S(2)}) %collective-permute-start.5) | collective-permute-done | bytes 262176 | tf_op jit(solution)/shard_map/ppermute | solution.py:424
  56.2 0.9 collective-permute-done.7.refs_1_
  57.9 4.9 %collective-permute-done.10.refs_0_ = bf16[1024,128]{1,0:T(8,128)(2,1)S(1)} collective-permute-done((bf16[1024,128]{1,0:T(8,128)(2,1)S(1)}, bf16[1024,128]{1,0:T(8,128)(2,1)S(1)}, u32[]{:S(2)}, u32[]{:S(2)}) %collective-permute-start.10) | collective-permute-done | bytes 262176 | tf_op jit(solution)/shard_map/ppermute | solution.py:421
  63.5 1.0 copy-done.2
  64.5 8.4 %expert.1 = (bf16[32,16,1024]{2,1,0:T(8,128)(2,1)}, bf16[8,2048,128]{2,1,0:T(8,128)(2,1)}) custom-call(s32[1]{0:T(128)} %bitcast.6.at_ref, bf16[32,16,1024]{2,1,0:T(8,128)(2,1)} %copy-done.2, bf16[1024,128]{1,0:T(8,128)(2,1)} %bitcast.61, bf16[1024,128]{1,0:T(8,128)(2,1)} %get-tuple-element.27.refs_1_, bf16[1024,128]{1,0:T(8,128)(2,1)} %copy-done.10, ...), custom_call_target="tpu_custom_call" | custom-call | flops 4000000000 | bytes 10485760 | tf_op jit(solution)/shard_map/expert/pallas_call | solution.py:228
  72.9 8.1 %all-to-all-start.1 = ((bf16[32,16,1024]{2,1,0:T(8,128)(2,1)}), bf16[32,16,1024]{2,1,0:T(8,128)(2,1)S(1)}, u32[]{:S(2)}, u32[]{:S(2)}) async-start(bf16[32,16,1024]{2,1,0:T(8,128)(2,1)} %get-tuple-element.35), calls=%async_computation.1 | async-start | bytes 2097152 | tf_op jit(solution)/shard_map/all_to_all | solution.py:449
  81.0 17.2 %all-to-all-done.1 = bf16[32,16,1024]{2,1,0:T(8,128)(2,1)S(1)} async-done(((bf16[32,16,1024]{2,1,0:T(8,128)(2,1)}), bf16[32,16,1024]{2,1,0:T(8,128)(2,1)S(1)}, u32[]{:S(2)}, u32[]{:S(2)}) %all-to-all-start.1) | async-done | bytes 1048608 | tf_op jit(solution)/shard_map/all_to_all | solution.py:449
  98.1 1.0 copy-done.3
  99.1 8.7 %route.1 = (f32[2,72,128]{2,1,0:T(8,128)}, bf16[1568,256]{1,0:T(8,128)(2,1)}, bf16[256,1024]{1,0:T(8,128)(2,1)}) custom-call(f32[1,1024]{1,0:T(1,128)} %bitcast.68, bf16[16,1024]{1,0:T(8,128)(2,1)} %bitcast.66, f32[8,128]{1,0:T(8,128)} %get-tuple-element.23.col_ref, bf16[1568,1024]{1,0:T(8,128)(2,1)} %bitcast.56, ...), custom_call_target="tpu_custom_call" | custom-call | flops 5000000000 | bytes 14680064 | tf_op jit(solution)/shard_map/route/pallas_call | solution.py:335
  109.1 0.9 collective-permute-done.14
  111.6 3.6 %all-to-all-start.2 = ((f32[16,72,128]{2,1,0:T(8,128)}), f32[16,72,128]{2,1,0:T(8,128)S(1)}, u32[]{:S(2)}, u32[]{:S(2)}) async-start(f32[16,72,128]{2,1,0:T(8,128)} %broadcast_in_dim.7), calls=%async_computation.2 | async-start | bytes 1179648 | tf_op jit(solution)/shard_map/all_to_all | solution.py:464
  115.2 6.8 %back.1.refs_1_ = bf16[1568,1024]{1,0:T(8,128)(2,1)} custom-call(f32[1,1024]{1,0:T(1,128)} %bitcast.69, bf16[256,1024]{1,0:T(8,128)(2,1)} %get-tuple-element.37.grad_ref, bf16[1568,1024]{1,0:T(8,128)(2,1)} %bitcast.58, bf16[1568,256]{1,0:T(8,128)(2,1)} %get-tuple-element.38.coef_ref), custom_call_target="tpu_custom_call" | custom-call | flops 5000000000 | bytes 8388608 | tf_op jit(solution)/shard_map/back/pallas_call | solution.py:374
  122.0 4.9 %all-to-all-done.2.refs_0_ = f32[16,72,128]{2,1,0:T(8,128)S(1)} async-done(((f32[16,72,128]{2,1,0:T(8,128)}), f32[16,72,128]{2,1,0:T(8,128)S(1)}, u32[]{:S(2)}, u32[]{:S(2)}) %all-to-all-start.2) | async-done | bytes 589856 | tf_op jit(solution)/shard_map/all_to_all | solution.py:464
  127.7 1.1 reduce_sum.18
  129.5 3.4 %all-to-all-start.3 = ((f32[8,72,128]{2,1,0:T(8,128)}), f32[8,72,128]{2,1,0:T(8,128)S(1)}, u32[]{:S(2)}, u32[]{:S(2)}) async-start(f32[8,72,128]{2,1,0:T(8,128)} %broadcast_in_dim.8), calls=%async_computation.3 | async-start | bytes 589824 | tf_op jit(solution)/shard_map/all_to_all | solution.py:464
  133.0 1.9 %fusion.1 = (f32[1,1024,128]{2,1,0:T(8,128)S(1)}, f32[1,1024,128]{2,1,0:T(8,128)}) fusion(bf16[1,2048,128]{2,1,0:T(8,128)(2,1)} %reduce-scatter.2.cloned.1.call-done), kind=kLoop, calls=%fused_computation.11 | loop fusion | bytes 2097152 | tf_op jit(solution)/shard_map/slice | solution.py:471
  135.2 0.9 copy.32
  136.1 7.4 %all-to-all-done.3.refs_0_ = f32[8,72,128]{2,1,0:T(8,128)S(1)} async-done(((f32[8,72,128]{2,1,0:T(8,128)}), f32[8,72,128]{2,1,0:T(8,128)S(1)}, u32[]{:S(2)}, u32[]{:S(2)}) %all-to-all-start.3) | async-done | bytes 294944 | tf_op jit(solution)/shard_map/all_to_all | solution.py:464
  144.2 1.0 reduce_sum.19
  145.2 3.1 %collective-permute-start.15 = (f32[72,128]{1,0:T(8,128)S(1)}, f32[72,128]{1,0:T(8,128)S(1)}, u32[]{:S(2)}, u32[]{:S(2)}) collective-permute-start(f32[72,128]{1,0:T(8,128)S(1)} %reduce_sum.19), channel_id=1, source_target_pairs={{0,1},{1,0},{2,3},{3,2},{4,5},{5,4},{6,7},{7,6},{8,9},{9,8},{10,11... | collective-permute-start | bytes 110600 | tf_op jit(solution)/shard_map/ppermute | solution.py:473
  148.2 0.9 broadcast_in_dim_reshape.3
  (68 shorter events, 9.2 us)
Async XLA Ops:
  7.2 17.9 %collective-permute-start = (bf16[1024,128]{1,0:T(8,128)(2,1)}, bf16[1024,128]{1,0:T(8,128)(2,1)S(1)}, u32[]{:S(2)}, u32[]{:S(2)}) collective-permute-start(bf16[1024,128]{1,0:T(8,128)(2,1)} %bitcast.59), channel_id=1, source_target_pairs={{0,112},{16,0},{32,16},{48,32},{64,48},{80,64},{96,80},{112,96},{1... | collective-permute-start | bytes 786440 | tf_op jit(solution)/shard_map/ppermute | solution.py:424
  13.6 11.5 %collective-permute-start.1 = (bf16[1024,128]{1,0:T(8,128)(2,1)}, bf16[1024,128]{1,0:T(8,128)(2,1)S(1)}, u32[]{:S(2)}, u32[]{:S(2)}) collective-permute-start(bf16[1024,128]{1,0:T(8,128)(2,1)} %bitcast.60), channel_id=1, source_target_pairs={{0,16},{16,32},{32,48},{48,64},{64,80},{80,96},{96,112},{112,0},{1... | collective-permute-start | bytes 786440 | tf_op jit(solution)/shard_map/ppermute | solution.py:421
  13.7 11.5 %collective-permute-start.2 = (bf16[128,1024]{1,0:T(8,128)(2,1)}, bf16[128,1024]{1,0:T(8,128)(2,1)S(1)}, u32[]{:S(2)}, u32[]{:S(2)}) collective-permute-start(bf16[128,1024]{1,0:T(8,128)(2,1)} %bitcast.62), channel_id=1, source_target_pairs={{0,112},{16,0},{32,16},{48,32},{64,48},{80,64},{96,80},{112,96},{1... | collective-permute-start | bytes 786440 | tf_op jit(solution)/shard_map/ppermute | solution.py:422
  16.3 11.2 %collective-permute-start.3 = (bf16[128,1024]{1,0:T(8,128)(2,1)}, bf16[128,1024]{1,0:T(8,128)(2,1)S(1)}, u32[]{:S(2)}, u32[]{:S(2)}) collective-permute-start(bf16[128,1024]{1,0:T(8,128)(2,1)} %bitcast.63), channel_id=1, source_target_pairs={{0,16},{16,32},{32,48},{48,64},{64,80},{80,96},{96,112},{112,0},{1... | collective-permute-start | bytes 786440 | tf_op jit(solution)/shard_map/ppermute | solution.py:425
  25.1 2.4 %copy-start.4 = (bf16[1024,128]{1,0:T(8,128)(2,1)}, bf16[1024,128]{1,0:T(8,128)(2,1)S(1)}, u32[]{:S(2)}) copy-start(bf16[1024,128]{1,0:T(8,128)(2,1)S(1)} %collective-permute-done.refs_1_) | copy-start | bytes 786436
  25.1 2.4 %copy-start.5 = (bf16[1024,128]{1,0:T(8,128)(2,1)}, bf16[1024,128]{1,0:T(8,128)(2,1)S(1)}, u32[]{:S(2)}) copy-start(bf16[1024,128]{1,0:T(8,128)(2,1)S(1)} %collective-permute-done.1.refs_2_) | copy-start | bytes 786436
  25.2 2.4 %copy-start.6 = (bf16[128,1024]{1,0:T(8,128)(2,1)}, bf16[128,1024]{1,0:T(8,128)(2,1)S(1)}, u32[]{:S(2)}) copy-start(bf16[128,1024]{1,0:T(8,128)(2,1)S(1)} %collective-permute-done.2.refs_3_) | copy-start | bytes 786436
  28.3 14.3 %collective-permute-start.8 = (bf16[1024,128]{1,0:T(8,128)(2,1)}, bf16[1024,128]{1,0:T(8,128)(2,1)S(1)}, u32[]{:S(2)}, u32[]{:S(2)}) collective-permute-start(bf16[1024,128]{1,0:T(8,128)(2,1)} %get-tuple-element.30.refs_7_), channel_id=1, source_target_pairs={{0,16},{16,32},{32,48},{48,64},{64,80},{80,96},{96,112},{112,0},{1... | collective-permute-start | bytes 786440 | tf_op jit(solution)/shard_map/ppermute | solution.py:421
  28.3 14.4 %collective-permute-start.11 = (bf16[128,1024]{1,0:T(8,128)(2,1)}, bf16[128,1024]{1,0:T(8,128)(2,1)S(1)}, u32[]{:S(2)}, u32[]{:S(2)}) collective-permute-start(bf16[128,1024]{1,0:T(8,128)(2,1)} %get-tuple-element.31.refs_9_), channel_id=1, source_target_pairs={{0,112},{16,0},{32,16},{48,32},{64,48},{80,64},{96,80},{112,96},{1... | collective-permute-start | bytes 786440 | tf_op jit(solution)/shard_map/ppermute | solution.py:422
  30.9 14.4 %collective-permute-start.4 = (bf16[1024,128]{1,0:T(8,128)(2,1)}, bf16[1024,128]{1,0:T(8,128)(2,1)S(1)}, u32[]{:S(2)}, u32[]{:S(2)}) collective-permute-start(bf16[1024,128]{1,0:T(8,128)(2,1)} %get-tuple-element.27.refs_1_), channel_id=1, source_target_pairs={{0,112},{16,0},{32,16},{48,32},{64,48},{80,64},{96,80},{112,96},{1... | collective-permute-start | bytes 786440 | tf_op jit(solution)/shard_map/ppermute | solution.py:424
  31.0 14.4 %collective-permute-start.6 = (bf16[128,1024]{1,0:T(8,128)(2,1)}, bf16[128,1024]{1,0:T(8,128)(2,1)S(1)}, u32[]{:S(2)}, u32[]{:S(2)}) collective-permute-start(bf16[128,1024]{1,0:T(8,128)(2,1)} %get-tuple-element.28.refs_15_), channel_id=1, source_target_pairs={{0,16},{16,32},{32,48},{48,64},{64,80},{80,96},{96,112},{112,0},{1... | collective-permute-start | bytes 786440 | tf_op jit(solution)/shard_map/ppermute | solution.py:425
  32.4 31.1 %all-to-all-start = ((bf16[32,16,1024]{2,1,0:T(8,128)(2,1)}), bf16[32,16,1024]{2,1,0:T(8,128)(2,1)S(1)}, u32[]{:S(2)}, u32[]{:S(2)}) async-start(bf16[32,16,1024]{2,1,0:T(8,128)(2,1)} %bitcast.46), calls=%async_computation | async-start | bytes 2097152 | tf_op jit(solution)/shard_map/all_to_all | solution.py:437
  42.5 90.5 %reduce-scatter.2.cloned.1.call-start = ((), (), s32[]{:S(2)}) async-start(), calls=%async_computation.5 | async-start | bytes 4718592 | tf_op jit(solution)/shard_map/reduce_scatter | solution.py:448
  42.5 15.3 %copy-start.8 = (bf16[1024,128]{1,0:T(8,128)(2,1)}, bf16[1024,128]{1,0:T(8,128)(2,1)S(1)}, u32[]{:S(2)}) copy-start(bf16[1024,128]{1,0:T(8,128)(2,1)S(1)} %collective-permute-done.8.refs_6_) | copy-start | bytes 786436
  42.5 9.0 %collective-permute-start.9 = (bf16[1024,128]{1,0:T(8,128)(2,1)S(1)}, bf16[1024,128]{1,0:T(8,128)(2,1)S(1)}, u32[]{:S(2)}, u32[]{:S(2)}) collective-permute-start(bf16[1024,128]{1,0:T(8,128)(2,1)S(1)} %collective-permute-done.8.refs_6_), channel_id=1, source_target_pairs={{0,16},{16,32},{32,48},{48,64},{64,80},{80,96},{96,112},{112,0},{1... | collective-permute-start | bytes 786440 | tf_op jit(solution)/shard_map/ppermute | solution.py:421
  42.6 15.2 %copy-start.9 = (bf16[128,1024]{1,0:T(8,128)(2,1)}, bf16[128,1024]{1,0:T(8,128)(2,1)S(1)}, u32[]{:S(2)}) copy-start(bf16[128,1024]{1,0:T(8,128)(2,1)S(1)} %collective-permute-done.11.refs_10_) | copy-start | bytes 786436
  42.7 8.9 %collective-permute-start.12 = (bf16[128,1024]{1,0:T(8,128)(2,1)S(1)}, bf16[128,1024]{1,0:T(8,128)(2,1)S(1)}, u32[]{:S(2)}, u32[]{:S(2)}) collective-permute-start(bf16[128,1024]{1,0:T(8,128)(2,1)S(1)} %collective-permute-done.11.refs_10_), channel_id=1, source_target_pairs={{0,112},{16,0},{32,16},{48,32},{64,48},{80,64},{96,80},{112,96},{1... | collective-permute-start | bytes 786440 | tf_op jit(solution)/shard_map/ppermute | solution.py:422
  45.3 12.5 %copy-start.10 = (bf16[1024,128]{1,0:T(8,128)(2,1)}, bf16[1024,128]{1,0:T(8,128)(2,1)S(1)}, u32[]{:S(2)}) copy-start(bf16[1024,128]{1,0:T(8,128)(2,1)S(1)} %collective-permute-done.4.refs_2_) | copy-start | bytes 786436
  45.3 10.9 %collective-permute-start.5 = (bf16[1024,128]{1,0:T(8,128)(2,1)S(1)}, bf16[1024,128]{1,0:T(8,128)(2,1)S(1)}, u32[]{:S(2)}, u32[]{:S(2)}) collective-permute-start(bf16[1024,128]{1,0:T(8,128)(2,1)S(1)} %collective-permute-done.4.refs_2_), channel_id=1, source_target_pairs={{0,112},{16,0},{32,16},{48,32},{64,48},{80,64},{96,80},{112,96},{1... | collective-permute-start | bytes 786440 | tf_op jit(solution)/shard_map/ppermute | solution.py:424
  45.4 12.4 %copy-start.11 = (bf16[128,1024]{1,0:T(8,128)(2,1)}, bf16[128,1024]{1,0:T(8,128)(2,1)S(1)}, u32[]{:S(2)}) copy-start(bf16[128,1024]{1,0:T(8,128)(2,1)S(1)} %collective-permute-done.6.refs_14_) | copy-start | bytes 786436
  45.4 11.7 %collective-permute-start.7 = (bf16[128,1024]{1,0:T(8,128)(2,1)S(1)}, bf16[128,1024]{1,0:T(8,128)(2,1)S(1)}, u32[]{:S(2)}, u32[]{:S(2)}) collective-permute-start(bf16[128,1024]{1,0:T(8,128)(2,1)S(1)} %collective-permute-done.6.refs_14_), channel_id=1, source_target_pairs={{0,16},{16,32},{32,48},{48,64},{64,80},{80,96},{96,112},{112,0},{1... | collective-permute-start | bytes 786440 | tf_op jit(solution)/shard_map/ppermute | solution.py:425
  51.5 6.3 %copy-start.12 = (bf16[1024,128]{1,0:T(8,128)(2,1)}, bf16[1024,128]{1,0:T(8,128)(2,1)S(1)}, u32[]{:S(2)}) copy-start(bf16[1024,128]{1,0:T(8,128)(2,1)S(1)} %collective-permute-done.9.refs_5_) | copy-start | bytes 786436
  51.5 11.2 %collective-permute-start.10 = (bf16[1024,128]{1,0:T(8,128)(2,1)S(1)}, bf16[1024,128]{1,0:T(8,128)(2,1)S(1)}, u32[]{:S(2)}, u32[]{:S(2)}) collective-permute-start(bf16[1024,128]{1,0:T(8,128)(2,1)S(1)} %collective-permute-done.9.refs_5_), channel_id=1, source_target_pairs={{0,16},{16,32},{32,48},{48,64},{64,80},{80,96},{96,112},{112,0},{1... | collective-permute-start | bytes 786440 | tf_op jit(solution)/shard_map/ppermute | solution.py:421
  51.5 6.3 %copy-start.13 = (bf16[128,1024]{1,0:T(8,128)(2,1)}, bf16[128,1024]{1,0:T(8,128)(2,1)S(1)}, u32[]{:S(2)}) copy-start(bf16[128,1024]{1,0:T(8,128)(2,1)S(1)} %collective-permute-done.12.refs_11_) | copy-start | bytes 786436
  51.5 11.2 %collective-permute-start.13 = (bf16[128,1024]{1,0:T(8,128)(2,1)S(1)}, bf16[128,1024]{1,0:T(8,128)(2,1)}, u32[]{:S(2)}, u32[]{:S(2)}) collective-permute-start(bf16[128,1024]{1,0:T(8,128)(2,1)S(1)} %collective-permute-done.12.refs_11_), channel_id=1, source_target_pairs={{0,112},{16,0},{32,16},{48,32},{64,48},{80,64},{96,80},{112,96},{1... | collective-permute-start | bytes 786440 | tf_op jit(solution)/shard_map/ppermute | solution.py:422
  63.5 1.0 copy-start.2
  72.9 25.3 %all-to-all-start.1 = ((bf16[32,16,1024]{2,1,0:T(8,128)(2,1)}), bf16[32,16,1024]{2,1,0:T(8,128)(2,1)S(1)}, u32[]{:S(2)}, u32[]{:S(2)}) async-start(bf16[32,16,1024]{2,1,0:T(8,128)(2,1)} %get-tuple-element.35), calls=%async_computation.1 | async-start | bytes 2097152 | tf_op jit(solution)/shard_map/all_to_all | solution.py:449
  98.1 1.0 copy-start.3
  108.7 1.3 collective-permute-start.14
  111.6 15.3 %all-to-all-start.2 = ((f32[16,72,128]{2,1,0:T(8,128)}), f32[16,72,128]{2,1,0:T(8,128)S(1)}, u32[]{:S(2)}, u32[]{:S(2)}) async-start(f32[16,72,128]{2,1,0:T(8,128)} %broadcast_in_dim.7), calls=%async_computation.2 | async-start | bytes 1179648 | tf_op jit(solution)/shard_map/all_to_all | solution.py:464
  129.5 13.9 %all-to-all-start.3 = ((f32[8,72,128]{2,1,0:T(8,128)}), f32[8,72,128]{2,1,0:T(8,128)S(1)}, u32[]{:S(2)}, u32[]{:S(2)}) async-start(f32[8,72,128]{2,1,0:T(8,128)} %broadcast_in_dim.8), calls=%async_computation.3 | async-start | bytes 589824 | tf_op jit(solution)/shard_map/all_to_all | solution.py:464
  145.2 3.9 %collective-permute-start.15 = (f32[72,128]{1,0:T(8,128)S(1)}, f32[72,128]{1,0:T(8,128)S(1)}, u32[]{:S(2)}, u32[]{:S(2)}) collective-permute-start(f32[72,128]{1,0:T(8,128)S(1)} %reduce_sum.19), channel_id=1, source_target_pairs={{0,1},{1,0},{2,3},{3,2},{4,5},{5,4},{6,7},{7,6},{8,9},{9,8},{10,11... | collective-permute-start | bytes 110600 | tf_op jit(solution)/shard_map/ppermute | solution.py:473
  (6 other events, 4.6 us)
Sparse Core Ops, SparseCore 0:
  73.0 53.8 reduce-scatter.1

commit v3 on v2

--- a/solution.py
+++ b/solution.py
@@ -14,6 +14,7 @@
 VMEM = 60 * 1024 * 1024
 RING = 3 * 10**9
 RING2 = 3 * 10**9
+LOW = 1024 * 1024
 
 
 def dot(a, b, ca, cb):
@@ -150,12 +151,12 @@
 gelu_k = 0.044715
 
 
-def expert_kernel(at_ref, act_ref, *refs):
-    n = (len(refs) - 14) // 2
+def expert_kernel(n, act_ref, *refs):
     firsts, seconds = refs[:n], refs[n : 2 * n]
+    ret_ref, dw_refs = refs[2 * n], refs[2 * n + 1 : 3 * n + 1]
     (
-        ret_ref, dw_ref, act_s, w1_s, w2_s, dw_s, ret_s, y_acc, g_acc, act_sem, w1_sem, w2_sem, dw_sem, ret_sem,
-    ) = refs[2 * n :]
+        act_s, w1_s, w2_s, dw_s, ret_s, y_acc, g_acc, act_sem, w1_sem, w2_sem, dw_sem, ret_sem,
+    ) = refs[3 * n + 1 :]
     peers, rows, features = act_s.shape
     half = rows // 2
     part = seconds[0].shape[0]
@@ -211,7 +212,7 @@
             dw_s[r, :features] = d_w1[:, mine]
             for j in range(features // part):
                 dw_s[r, pl.ds(features + j * part, part)] = d_w2[mine, j * part : (j + 1) * part]
-            send = pltpu.make_async_copy(dw_s.at[r], dw_ref.at[lax.rem(at_ref[0] + r, n)], dw_sem.at[r])
+            send = pltpu.make_async_copy(dw_s.at[r], dw_refs[r], dw_sem.at[r])
             send.start()
             sends.append(send)
     ret_copy.wait()
@@ -219,24 +220,24 @@
         send.wait()
 
 
-def expert(at, act, firsts, seconds):
+def expert(act, firsts, seconds):
     peers, rows, features = act.shape
     part = firsts[0].shape[1]
     n = len(firsts)
     all_rows = peers * rows // 2
-    size = 2
-    return pl.pallas_call(
-        expert_kernel,
-        in_specs=[pl.BlockSpec(memory_space=pltpu.SMEM)] + [anywhere] * (1 + 2 * n),
-        out_specs=[anywhere, anywhere],
-        out_shape=[
-            jax.ShapeDtypeStruct((peers, rows, features), bf16),
-            jax.ShapeDtypeStruct((n, 2 * features, part), bf16),
-        ],
+    size = 4 if n % 4 == 0 else 1
+    wide = pltpu.VMEM((n // size, features, size * part), bf16)
+    tall = pltpu.VMEM((n // size, size * part, features), bf16)
+    got = pl.pallas_call(
+        functools.partial(expert_kernel, n),
+        in_specs=[anywhere] * (1 + 2 * n),
+        out_specs=[anywhere] * (1 + n),
+        out_shape=[jax.ShapeDtypeStruct(act.shape, bf16)]
+        + [jax.ShapeDtypeStruct((2 * features, part), bf16)] * n,
         scratch_shapes=[
             pltpu.VMEM((peers, rows, features), bf16),
-            pltpu.VMEM((n // size, features, size * part), bf16),
-            pltpu.VMEM((n // size, size * part, features), bf16),
+            wide,
+            tall,
             pltpu.VMEM((n, 2 * features, part), bf16),
             pltpu.VMEM((peers, rows, features), bf16),
             pltpu.VMEM((all_rows, features), f32),
@@ -250,12 +251,34 @@
         compiler_params=pltpu.CompilerParams(vmem_limit_bytes=VMEM),
         cost_estimate=pl.CostEstimate(flops=4 * 10**9, bytes_accessed=10 * 2**20, transcendentals=10**6),
         name="expert",
-    )(at, act, *firsts, *seconds)
+    )(act, *firsts, *seconds)
+    return got[0], got[1:]
+
+
+def add_up_kernel(*refs):
+    total = 0.0
+    for ref in refs[:-1]:
+        for k in range(ref.shape[0]):
+            total = total + ref[k]
+    for k in range(refs[-1].shape[0]):
+        refs[-1][k] = total
+
+
+def add_up(arrays, copies):
+    return pl.pallas_call(
+        add_up_kernel,
+        in_specs=[vmem] * len(arrays),
+        out_specs=vmem,
+        out_shape=jax.ShapeDtypeStruct((copies, *arrays[0].shape[1:]), f32),
+        compiler_params=pltpu.CompilerParams(vmem_limit_bytes=8 * 1024 * 1024),
+        cost_estimate=pl.CostEstimate(flops=10**8, bytes_accessed=2**20, transcendentals=0),
+        name="add_up",
+    )(*arrays)
 
 
 def route_kernel(
-    shares, gain_ref, slot_ref, col_ref, c_ref, normed_ref, ret_ref, acc_ref,
-    sums_ref, coef_ref, grad_ref,
+    shares, core_ref, gain_ref, slot_ref, col_ref, c_ref, normed_ref, ret_ref, acc_ref,
+    mine_ref, other_ref, coef_ref, grad_ref,
     c_s, normed_s, ret_s, acc_s, coef_s, grad_s, out_s, pd_s, dd_s, fc_s,
     c_sem, normed_sem, whole_sem, coef_sem,
 ):
@@ -269,12 +292,10 @@
     ret_in = pltpu.make_async_copy(ret_ref, ret_s, whole_sem.at[0])
     acc_in = pltpu.make_async_copy(acc_ref, acc_s, whole_sem.at[1])
     grad_out = pltpu.make_async_copy(grad_s, grad_ref, whole_sem.at[2])
-    normed_in[0].start()
     ret_in.start()
-    c_in[0].start()
-    for k in range(1, len(slices)):
-        normed_in[k].start()
-        c_in[k].start()
+    for one, two in zip(normed_in, c_in):
+        one.start()
+        two.start()
     acc_in.start()
     wrep = replicated(slot_ref, images)
     grad_s[wide:] = wrep
@@ -310,33 +331,40 @@
     d_gain = jnp.sum(acc_s[...] * grad_s[:wide].astype(f32), axis=0, keepdims=True)
     d_gain = d_gain + jnp.sum(acc * grad_s[wide:].astype(f32), axis=0, keepdims=True)
     d_gain = d_gain / gain_ref[...]
-    pieces, _, part = sums_ref.shape
-    blocks = features // part // pieces
-    for k in range(pieces):
-        start = k * blocks * part
-        for j in range(blocks):
-            sums_ref[k, j * slots : (j + 1) * slots] = d_weight[:, start + j * part : start + (j + 1) * part]
-        last = [d_gain[:, start + j * part : start + (j + 1) * part] for j in range(blocks)]
-        last.append(jnp.zeros((8 - blocks, part), f32))
-        sums_ref[k, blocks * slots :] = jnp.concatenate(last, axis=0)
+    part = mine_ref.shape[1]
+    blocks = features // part // 2
+    first = core_ref[0] == 0
+
+    def chosen(j, rows):
+        low = rows[:, j * part : (j + 1) * part]
+        high = rows[:, (blocks + j) * part : (blocks + j + 1) * part]
+        return jnp.where(first, low, high), jnp.where(first, high, low)
+
+    for j in range(blocks):
+        here = slice(j * slots, (j + 1) * slots)
+        mine_ref[here], other_ref[here] = chosen(j, d_weight)
+    last = [chosen(j, d_gain) for j in range(blocks)]
+    rest = jnp.zeros((8 - blocks, part), f32)
+    mine_ref[blocks * slots :] = jnp.concatenate([one for one, _ in last] + [rest], axis=0)
+    other_ref[blocks * slots :] = jnp.concatenate([two for _, two in last] + [rest], axis=0)
     for copy in coef_out:
         copy.wait()
     grad_out.wait()
 
 
-def route(cotangent, normed, norm_gain, slot_t, col, ret, acc, pieces, shares=(1, 1)):
+def route(core, cotangent, normed, norm_gain, slot_t, col, ret, acc, shares=(1, 1)):
     rows, features = cotangent.shape
     _, slots, images, _ = ret.shape
     wide = slots * images // 2
     n = len(shares)
     ins = (cotangent, normed, ret, acc)
     outs = [((rows, 2 * wide), bf16), ((2 * wide, features), bf16)]
-    sums = jax.ShapeDtypeStruct((pieces, features // 128 // pieces * slots + 8, 128), f32)
+    sums = jax.ShapeDtypeStruct((features // 256 * slots + 8, 128), f32)
     return pl.pallas_call(
         functools.partial(route_kernel, shares),
-        in_specs=[vmem] * 3 + [anywhere] * len(ins),
-        out_specs=[vmem] + [anywhere] * len(outs),
-        out_shape=[sums] + [jax.ShapeDtypeStruct(*out) for out in outs],
+        in_specs=[pl.BlockSpec(memory_space=pltpu.SMEM)] + [vmem] * 3 + [anywhere] * len(ins),
+        out_specs=[vmem] * 2 + [anywhere] * len(outs),
+        out_shape=[sums] * 2 + [jax.ShapeDtypeStruct(*out) for out in outs],
         scratch_shapes=[pltpu.VMEM(x.shape, x.dtype) for x in ins]
         + [pltpu.VMEM(*out) for out in outs]
         + [
@@ -352,7 +380,7 @@
         compiler_params=pltpu.CompilerParams(vmem_limit_bytes=VMEM),
         cost_estimate=pl.CostEstimate(flops=5 * 10**9, bytes_accessed=14 * 2**20, transcendentals=0),
         name="route",
-    )(norm_gain, slot_t, col, *ins)
+    )(core, norm_gain, slot_t, col, *ins)
 
 
 def back_kernel(gain_ref, grad_ref, x_ref, coef_ref, dt_ref):
@@ -392,13 +420,14 @@
     pass
 
 
-def after(kept, others, weight=0):
+def after(kept, others, weight=0, limit=None):
     return pl.pallas_call(
         gate_kernel,
         in_specs=[anywhere] * (len(kept) + len(others)),
         out_specs=[anywhere] * len(kept),
         out_shape=[jax.ShapeDtypeStruct(x.shape, x.dtype) for x in kept],
         input_output_aliases={i: i for i in range(len(kept))},
+        compiler_params=pltpu.CompilerParams(vmem_limit_bytes=limit),
         cost_estimate=pl.CostEstimate(flops=weight, bytes_accessed=0, transcendentals=0),
         name="after",
     )(*kept, *others)
@@ -443,37 +472,51 @@
     firsts[far], seconds[far] = after([firsts[far], seconds[far]], [], RING)
     if n > 3:
         firsts[far - 1], seconds[far + 1] = after([firsts[far - 1], seconds[far + 1]], [], RING2)
-    at = lax.axis_index("z").reshape(1)
-    ret, d_w = expert(at, act, [firsts[r] for r in range(n)], [seconds[r] for r in range(n)])
-    d_w = lax.psum_scatter(d_w, "z", scatter_dimension=0, tiled=False).astype(f32)
+    ret, d_w = expert(act, [firsts[r] for r in range(n)], [seconds[r] for r in range(n)])
     ret = lax.all_to_all(ret, peers, 0, 0, tiled=True)
-    cores = lax.axis_size("c")
-    ret = ret.reshape(halves, slots, 2 * images, features)
-    sums, coef, grad = route(cots, normed, gain, slot_t, col, ret, acc, cores)
+
+    state = [d_w[far], d_w[(far + 1) % n]]
+
+    def pass_on(k):
+        state[0] = lax.ppermute(state[0], "z", up)
+        if k < far:
+            state[1] = lax.ppermute(state[1], "z", down)
+
+    def add_own(k):
+        state[0] = state[0] + d_w[far - k]
+        if k < far - 1:
+            state[1] = state[1] + d_w[far + 1 + k]
+
+    pass_on(1)
+    if far > 2:
+        add_own(1)
+        pass_on(2)
+    done = 2 if far > 2 else 1
 
     core = lax.axis_index("c")
     swap = [(0, 1), (1, 0)]
-    other = lax.ppermute(lax.dynamic_index_in_dim(sums, 1 - core, 0, False), "c", swap)
-    share = lax.dynamic_index_in_dim(sums, core, 0, False) + other
-
-    def total(share, axes, others=()):
-        many = 1
-        for axis in axes:
-            many *= lax.axis_size(axis)
-        copies = jnp.broadcast_to(share[None], (many, *share.shape))
-        (copies,) = after([lax.all_to_all(copies, axes, 0, 0, tiled=True)], others)
-        return jnp.sum(copies, axis=0)
-
-    d_tokens = back(by_place, coef, gain, grad)
-    share = total(share, ("yh", "yl", "x"), [d_tokens])
+    ret = ret.reshape(halves, slots, 2 * images, features)
+    mine, other, coef, grad = route(core.reshape(1), cots, normed, gain, slot_t, col, ret, acc)
+    plane = ("yh", "yl", "x")
+    n_plane = halves * lax.axis_size("yl") * lax.axis_size("x")
+    copies = add_up([mine[None], lax.ppermute(other, "c", swap)[None]], n_plane)
+    state = list(after(state, [copies], limit=LOW))
+    copies = lax.all_to_all(copies, plane, 0, 0, tiled=True)
+    for k in range(done, far):
+        add_own(k)
+        pass_on(k + 1)
+    copies = add_up([copies], n)
+    (late_gain,) = after([gain], [copies], limit=LOW)
+    d_tokens = back(by_place, coef, late_gain, grad)
+    (share,) = add_up([lax.all_to_all(copies, "z", 0, 0, tiled=True)], 1)
     pieces = features // part
-    d_first = d_w[:features]
-    d_second = d_w[features:].reshape(pieces, part, part).swapaxes(0, 1).reshape(part, features)
-    share = total(share, ("z",), [d_first, d_second])
+    total = (d_w[0].astype(f32) + state[0].astype(f32)) + state[1].astype(f32)
+    d_first = total[:features]
+    d_second = total[features:].reshape(pieces, part, part).swapaxes(0, 1).reshape(part, features)
     other = lax.ppermute(share, "c", swap)
     sums = jnp.stack([jnp.where(core == 0, share, other), jnp.where(core == 0, other, share)])
-    blocks = features // sums.shape[2] // cores
-    d_slot_weight = sums[:, : blocks * slots].reshape(cores * blocks, slots, -1)
+    blocks = features // sums.shape[2] // 2
+    d_slot_weight = sums[:, : blocks * slots].reshape(2 * blocks, slots, -1)
     d_slot_weight = d_slot_weight.swapaxes(0, 1).reshape(slots, features).T
     d_gain = sums[:, blocks * slots : blocks * slots + blocks].reshape(features)
     d_tokens = d_tokens.reshape(tok, images, features).swapaxes(0, 1)

time: 158 us -> 152 us (0.962)
  starting transfers between devices: 48.9 us -> 65.4 us
  between operations: 14.3 us -> 0.93 us
  waiting for transfers between devices: 45.3 us -> 35.1 us
  local copies, waits for them, and re-layouts: 12.7 us -> 9.54 us
  other arithmetic: 3.47 us -> 5.97 us
    all_to_all x1, waiting for transfers between devices: 17.2 us -> 0.01 us  [on_device(): ret = lax.all_to_all(ret, peers, 0, 0, tiled=True)]
    ppermute x1 -> x8, waiting for transfers between devices: 0.87 us -> 16.1 us  [the longest x3 11.4 us: pass_on(): state[1] = lax.ppermute(state[1], 'z', down)]
    ppermute x1 -> x8, starting transfers between devices: 0.43 us -> 9.99 us  [the longest x3 8.56 us: pass_on(): state[1] = lax.ppermute(state[1], 'z', down)]
    all_to_all x2, waiting for transfers between devices: 12.3 us -> 4.09 us  [the longest x1 2.36 us: on_device(): share, = add_up([lax.all_to_all(copies, 'z', 0, 0, tiled=True)], 1)]
    all_to_all x2, starting transfers between devices: 7 us -> 12.7 us  [the longest x1 6.82 us: on_device(): copies = lax.all_to_all(copies, plane, 0, 0, tiled=True)]
    add x1 -> x6, other arithmetic: 0.77 us -> 5.36 us  [the longest x3 3.86 us: add_own(): state[0] = state[0] + d_w[far - k]]
    reduce_sum x2 -> x0, other arithmetic: 2.09 us -> none  [total(): return jnp.sum(copies, axis=0)]
    broadcast_in_dim x2 -> x0, local copies, waits for them, and re-layouts: 1.61 us -> none  [total(): copies = jnp.broadcast_to(share[None], (many, *share.shape))]
  transfers between devices with their start and end apart: 21 -> 27, of which waited for: 9 -> 10; matrix products, arithmetic and copies ran while one was open for 5% -> 4% of each run, Pallas kernels for 15% -> 17%
where the time goes in v3:
time: 152 us; the launch traced here: 151 us
  starting transfers between devices  65.4 us (43%)
  waiting for transfers between devices  35.1 us (23%)
  Pallas kernels  33.7 us (22%)
  local copies, waits for them, and re-layouts  9.54 us (6%)
  other arithmetic  5.97 us (4%)
    ppermute x3, waiting for transfers between devices, pass_on(): state[1] = lax.ppermute(state[1], 'z', down)  11.4 us
    ppermute x4, starting transfers between devices, step(): seconds[k] = lax.ppermute(seconds[k - 1], 'z', down)  10.7 us
    all_to_all x1, starting transfers between devices, on_device(): lax.all_to_all(sent.reshape(halves * slots, 2 * images, features), peers,...  10.1 us
    ppermute x4, waiting for transfers between devices, step(): firsts[n - k] = lax.ppermute(firsts[(n - k + 1) % n], 'z', up)  9.6 us
    pallas_call x1, Pallas kernels, front(): pl.pallas_call(functools.partial(front_kernel, shares), in_specs=[vmem, v...  8.77 us
    pallas_call x1, Pallas kernels, route(): pl.pallas_call(functools.partial(route_kernel, shares), in_specs=[pl.Bloc...  8.69 us
    ppermute x3, starting transfers between devices, pass_on(): state[1] = lax.ppermute(state[1], 'z', down)  8.56 us
    all_to_all x1, starting transfers between devices, on_device(): ret = lax.all_to_all(ret, peers, 0, 0, tiled=True)  8.21 us
  transfers between devices with their start and end apart: 27, of which 10 were waited for; matrix products, arithmetic and copies ran while one was open for 4% of the time, Pallas kernels for 17%

profile of v3, /device:TPU:1, one launch (start us, length us, event | category | flops | bytes accessed | tf_op | source)
XLA Modules:
  0.0 150.7 jit_solution(16368166042515294026)
XLA Ops:
  0.6 1.3 copy.41
  1.9 6.4 %collective-permute-start = (bf16[1024,128]{1,0:T(8,128)(2,1)}, bf16[1024,128]{1,0:T(8,128)(2,1)S(1)}, u32[]{:S(2)}, u32[]{:S(2)}) collective-permute-start(bf16[1024,128]{1,0:T(8,128)(2,1)} %bitcast.57), channel_id=1, source_target_pairs={{0,112},{16,0},{32,16},{48,32},{64,48},{80,64},{96,80},{112,96},{1... | collective-permute-start | bytes 786440 | tf_op jit(solution)/shard_map/ppermute | solution.py:453
  8.3 2.7 %collective-permute-start.2 = (bf16[128,1024]{1,0:T(8,128)(2,1)}, bf16[128,1024]{1,0:T(8,128)(2,1)S(1)}, u32[]{:S(2)}, u32[]{:S(2)}) collective-permute-start(bf16[128,1024]{1,0:T(8,128)(2,1)} %bitcast.60), channel_id=1, source_target_pairs={{0,112},{16,0},{32,16},{48,32},{64,48},{80,64},{96,80},{112,96},{1... | collective-permute-start | bytes 786440 | tf_op jit(solution)/shard_map/ppermute | solution.py:451
  11.0 8.8 %front.1 = (bf16[2,16,16,1024]{3,2,1,0:T(8,128)(2,1)}, bf16[1568,1024]{1,0:T(8,128)(2,1)}, f32[128,1024]{1,0:T(8,128)}, f32[8,128]{1,0:T(8,128)}) custom-call(f32[1,1024]{1,0:T(1,128)} %bitcast.44, bf16[16,1024]{1,0:T(8,128)(2,1)} %bitcast.63, bf16[1568,1024]{1,0:T(8,128)(2,1)} %bitcast.55, bf16[1568,1024]{1,0:T(8,128)(2,1)} %bitcast.53), custom_call_target="tpu_custom_call" | custom-call | flops 8000000000 | bytes 14680064 | tf_op jit(solution)/shard_map/front/pallas_call | solution.py:123
  19.8 2.4 %collective-permute-done.3.refs_4_ = bf16[128,1024]{1,0:T(8,128)(2,1)S(1)} collective-permute-done((bf16[128,1024]{1,0:T(8,128)(2,1)}, bf16[128,1024]{1,0:T(8,128)(2,1)S(1)}, u32[]{:S(2)}, u32[]{:S(2)}) %collective-permute-start.3) | collective-permute-done | bytes 262176 | tf_op jit(solution)/shard_map/ppermute | solution.py:454
  23.0 2.7 %collective-permute-start.11 = (bf16[128,1024]{1,0:T(8,128)(2,1)}, bf16[128,1024]{1,0:T(8,128)(2,1)S(1)}, u32[]{:S(2)}, u32[]{:S(2)}) collective-permute-start(bf16[128,1024]{1,0:T(8,128)(2,1)} %get-tuple-element.41.refs_9_), channel_id=1, source_target_pairs={{0,112},{16,0},{32,16},{48,32},{64,48},{80,64},{96,80},{112,96},{1... | collective-permute-start | bytes 786440 | tf_op jit(solution)/shard_map/ppermute | solution.py:451
  25.7 1.4 collective-permute-start.6
  27.1 10.1 %all-to-all-start = ((bf16[32,16,1024]{2,1,0:T(8,128)(2,1)}), bf16[32,16,1024]{2,1,0:T(8,128)(2,1)S(1)}, u32[]{:S(2)}, u32[]{:S(2)}) async-start(bf16[32,16,1024]{2,1,0:T(8,128)(2,1)} %bitcast.47), calls=%async_computation | async-start | bytes 2097152 | tf_op jit(solution)/shard_map/all_to_all | solution.py:466
  37.3 2.6 %collective-permute-start.12 = (bf16[128,1024]{1,0:T(8,128)(2,1)S(1)}, bf16[128,1024]{1,0:T(8,128)(2,1)S(1)}, u32[]{:S(2)}, u32[]{:S(2)}) collective-permute-start(bf16[128,1024]{1,0:T(8,128)(2,1)S(1)} %collective-permute-done.11.refs_10_), channel_id=1, source_target_pairs={{0,112},{16,0},{32,16},{48,32},{64,48},{80,64},{96,80},{112,96},{1... | collective-permute-start | bytes 786440 | tf_op jit(solution)/shard_map/ppermute | solution.py:451
  40.1 1.4 collective-permute-start.7
  41.4 4.7 %collective-permute-done.9.refs_5_ = bf16[1024,128]{1,0:T(8,128)(2,1)S(1)} collective-permute-done((bf16[1024,128]{1,0:T(8,128)(2,1)S(1)}, bf16[1024,128]{1,0:T(8,128)(2,1)S(1)}, u32[]{:S(2)}, u32[]{:S(2)}) %collective-permute-start.9) | collective-permute-done | bytes 262176 | tf_op jit(solution)/shard_map/ppermute | solution.py:450
  46.2 2.7 %collective-permute-start.13 = (bf16[128,1024]{1,0:T(8,128)(2,1)S(1)}, bf16[128,1024]{1,0:T(8,128)(2,1)}, u32[]{:S(2)}, u32[]{:S(2)}) collective-permute-start(bf16[128,1024]{1,0:T(8,128)(2,1)S(1)} %collective-permute-done.12.refs_11_), channel_id=1, source_target_pairs={{0,112},{16,0},{32,16},{48,32},{64,48},{80,64},{96,80},{112,96},{1... | collective-permute-start | bytes 786440 | tf_op jit(solution)/shard_map/ppermute | solution.py:451
  48.8 2.0 %collective-permute-done.5.refs_0_ = bf16[1024,128]{1,0:T(8,128)(2,1)S(1)} collective-permute-done((bf16[1024,128]{1,0:T(8,128)(2,1)S(1)}, bf16[1024,128]{1,0:T(8,128)(2,1)S(1)}, u32[]{:S(2)}, u32[]{:S(2)}) %collective-permute-start.5) | collective-permute-done | bytes 262176 | tf_op jit(solution)/shard_map/ppermute | solution.py:453
  52.5 4.9 %collective-permute-done.10.refs_0_ = bf16[1024,128]{1,0:T(8,128)(2,1)S(1)} collective-permute-done((bf16[1024,128]{1,0:T(8,128)(2,1)S(1)}, bf16[1024,128]{1,0:T(8,128)(2,1)S(1)}, u32[]{:S(2)}, u32[]{:S(2)}) %collective-permute-start.10) | collective-permute-done | bytes 262176 | tf_op jit(solution)/shard_map/ppermute | solution.py:450
  59.1 7.8 %expert.1 = (bf16[32,16,1024]{2,1,0:T(8,128)(2,1)}, bf16[2048,128]{1,0:T(8,128)(2,1)}, bf16[2048,128]{1,0:T(8,128)(2,1)}, bf16[2048,128]{1,0:T(8,128)(2,1)}, bf1...) custom-call(bf16[32,16,1024]{2,1,0:T(8,128)(2,1)} %copy-done.3, ...), custom_call_target="tpu_custom_call" | custom-call | flops 4000000000 | bytes 10485760 | tf_op jit(solution)/shard_map/expert/pallas_call | solution.py:231
  67.0 8.2 %all-to-all-start.1 = ((bf16[32,16,1024]{2,1,0:T(8,128)(2,1)}), bf16[32,16,1024]{2,1,0:T(8,128)(2,1)S(1)}, u32[]{:S(2)}, u32[]{:S(2)}) async-start(bf16[32,16,1024]{2,1,0:T(8,128)(2,1)} %get-tuple-element.45), calls=%async_computation.1 | async-start | bytes 2097152 | tf_op jit(solution)/shard_map/all_to_all | solution.py:476
  75.2 2.2 %collective-permute-start.18 = (bf16[2048,128]{1,0:T(8,128)(2,1)}, bf16[2048,128]{1,0:T(8,128)(2,1)S(1)}, u32[]{:S(2)}, u32[]{:S(2)}) collective-permute-start(bf16[2048,128]{1,0:T(8,128)(2,1)} %get-tuple-element.54), channel_id=1, source_target_pairs={{0,112},{16,0},{32,16},{48,32},{64,48},{80,64},{96,80},{112,96},{1... | collective-permute-start | bytes 1572872 | tf_op jit(solution)/shard_map/ppermute | solution.py:483
  77.3 11.4 %collective-permute-done.18 = bf16[2048,128]{1,0:T(8,128)(2,1)S(1)} collective-permute-done((bf16[2048,128]{1,0:T(8,128)(2,1)}, bf16[2048,128]{1,0:T(8,128)(2,1)S(1)}, u32[]{:S(2)}, u32[]{:S(2)}) %collective-permute-start.18) | collective-permute-done | bytes 524320 | tf_op jit(solution)/shard_map/ppermute | solution.py:483
  88.8 1.2 add.22
  89.9 3.4 %collective-permute-start.19 = (bf16[2048,128]{1,0:T(8,128)(2,1)S(1)}, bf16[2048,128]{1,0:T(8,128)(2,1)S(1)}, u32[]{:S(2)}, u32[]{:S(2)}) collective-permute-start(bf16[2048,128]{1,0:T(8,128)(2,1)S(1)} %add.22), channel_id=1, source_target_pairs={{0,112},{16,0},{32,16},{48,32},{64,48},{80,64},{96,80},{112,96},{1... | collective-permute-start | bytes 1572872 | tf_op jit(solution)/shard_map/ppermute | solution.py:483
  95.3 8.7 %route.1 = (f32[72,128]{1,0:T(8,128)}, f32[72,128]{1,0:T(8,128)}, bf16[1568,256]{1,0:T(8,128)(2,1)}, bf16[256,1024]{1,0:T(8,128)(2,1)}) custom-call(s32[1]{0:T(128)} %bitcast.1.core_ref, f32[1,1024]{1,0:T(1,128)} %bitcast.45, bf16[16,1024]{1,0:T(8,128)(2,1)} %bitcast.64, f32[8,128]{1,0:T(8,128)} %get-tuple-element.33.col_ref, bf16[1568,1024]{1,0:T(8,128)(2,1)} %bitcast.54, ...), custom_call_target="tpu_custom_call" | custom-call | flops 5000000000 | bytes 14680064 | tf_op jit(solution)/shard_map/route/pallas_call | solution.py:363
  104.0 1.4 collective-permute-start.14
  105.4 1.1 collective-permute-done.14
  109.1 6.8 %all-to-all-start.2 = ((f32[16,72,128]{2,1,0:T(8,128)}), f32[16,72,128]{2,1,0:T(8,128)S(1)}, u32[]{:S(2)}, u32[]{:S(2)}) async-start(f32[16,72,128]{2,1,0:T(8,128)} %add_up.3.refs_2_), calls=%async_computation.2 | async-start | bytes 1179648 | tf_op jit(solution)/shard_map/all_to_all | solution.py:504
  116.1 3.0 %collective-permute-start.22 = (bf16[2048,128]{1,0:T(8,128)(2,1)S(1)}, bf16[2048,128]{1,0:T(8,128)(2,1)S(1)}, u32[]{:S(2)}, u32[]{:S(2)}) collective-permute-start(bf16[2048,128]{1,0:T(8,128)(2,1)S(1)} %add.26), channel_id=1, source_target_pairs={{0,112},{16,0},{32,16},{48,32},{64,48},{80,64},{96,80},{112,96},{1... | collective-permute-start | bytes 1572872 | tf_op jit(solution)/shard_map/ppermute | solution.py:483
  119.1 3.6 %collective-permute-done.20 = bf16[2048,128]{1,0:T(8,128)(2,1)} collective-permute-done((bf16[2048,128]{1,0:T(8,128)(2,1)}, bf16[2048,128]{1,0:T(8,128)(2,1)}, u32[]{:S(2)}, u32[]{:S(2)}) %collective-permute-start.20) | collective-permute-done | bytes 524320 | tf_op jit(solution)/shard_map/ppermute | solution.py:481
  122.7 2.0 %add.24 = bf16[2048,128]{1,0:T(8,128)(2,1)} add(bf16[2048,128]{1,0:T(8,128)(2,1)} %collective-permute-done.20, bf16[2048,128]{1,0:T(8,128)(2,1)S(1)} %copy-done.6) | non-fusion elementwise | flops 262144 | bytes 1572864 | tf_op jit(solution)/shard_map/add | solution.py:486
  124.7 1.7 %all-to-all-done.2.refs_0_ = f32[16,72,128]{2,1,0:T(8,128)S(1)} async-done(((f32[16,72,128]{2,1,0:T(8,128)}), f32[16,72,128]{2,1,0:T(8,128)S(1)}, u32[]{:S(2)}, u32[]{:S(2)}) %all-to-all-start.2) | async-done | bytes 589856 | tf_op jit(solution)/shard_map/all_to_all | solution.py:504
  127.2 5.9 %all-to-all-start.3 = ((f32[8,72,128]{2,1,0:T(8,128)}), f32[8,72,128]{2,1,0:T(8,128)S(1)}, u32[]{:S(2)}, u32[]{:S(2)}) async-start(f32[8,72,128]{2,1,0:T(8,128)} %add_up.4.refs_1_), calls=%async_computation.3 | async-start | bytes 589824 | tf_op jit(solution)/shard_map/all_to_all | solution.py:511
  133.7 6.8 %back.1 = bf16[1568,1024]{1,0:T(8,128)(2,1)} custom-call(f32[1,1024]{1,0:T(1,128)} %copy-done.2, bf16[256,1024]{1,0:T(8,128)(2,1)} %get-tuple-element.49.grad_ref, bf16[1568,1024]{1,0:T(8,128)(2,1)} %bitcast.56, bf16[1568,256]{1,0:T(8,128)(2,1)} %get-tuple-element.50.coef_ref), custom_call_target="tpu_custom_call" | custom-call | flops 5000000000 | bytes 8388608 | tf_op jit(solution)/shard_map/back/pallas_call | solution.py:402
  140.7 2.4 %all-to-all-done.3.refs_0_ = f32[8,72,128]{2,1,0:T(8,128)S(1)} async-done(((f32[8,72,128]{2,1,0:T(8,128)}), f32[8,72,128]{2,1,0:T(8,128)S(1)}, u32[]{:S(2)}, u32[]{:S(2)}) %all-to-all-start.3) | async-done | bytes 294944 | tf_op jit(solution)/shard_map/all_to_all | solution.py:511
  143.1 4.3 %collective-permute-start.15 = (f32[72,128]{1,0:T(8,128)S(1)}, f32[72,128]{1,0:T(8,128)S(1)}, u32[]{:S(2)}, u32[]{:S(2)}) collective-permute-start(f32[72,128]{1,0:T(8,128)S(1)} %bitcast.41), channel_id=1, source_target_pairs={{0,1},{1,0},{2,3},{3,2},{4,5},{5,4},{6,7},{7,6},{8,9},{9,8},{10,11... | collective-permute-start | bytes 110600 | tf_op jit(solution)/shard_map/ppermute | solution.py:516
  (94 shorter events, 13.9 us)
Async XLA Ops:
  1.9 17.9 %collective-permute-start = (bf16[1024,128]{1,0:T(8,128)(2,1)}, bf16[1024,128]{1,0:T(8,128)(2,1)S(1)}, u32[]{:S(2)}, u32[]{:S(2)}) collective-permute-start(bf16[1024,128]{1,0:T(8,128)(2,1)} %bitcast.57), channel_id=1, source_target_pairs={{0,112},{16,0},{32,16},{48,32},{64,48},{80,64},{96,80},{112,96},{1... | collective-permute-start | bytes 786440 | tf_op jit(solution)/shard_map/ppermute | solution.py:453
  8.3 11.5 %collective-permute-start.1 = (bf16[1024,128]{1,0:T(8,128)(2,1)}, bf16[1024,128]{1,0:T(8,128)(2,1)S(1)}, u32[]{:S(2)}, u32[]{:S(2)}) collective-permute-start(bf16[1024,128]{1,0:T(8,128)(2,1)} %bitcast.58), channel_id=1, source_target_pairs={{0,16},{16,32},{32,48},{48,64},{64,80},{80,96},{96,112},{112,0},{1... | collective-permute-start | bytes 786440 | tf_op jit(solution)/shard_map/ppermute | solution.py:450
  8.3 11.5 %collective-permute-start.2 = (bf16[128,1024]{1,0:T(8,128)(2,1)}, bf16[128,1024]{1,0:T(8,128)(2,1)S(1)}, u32[]{:S(2)}, u32[]{:S(2)}) collective-permute-start(bf16[128,1024]{1,0:T(8,128)(2,1)} %bitcast.60), channel_id=1, source_target_pairs={{0,112},{16,0},{32,16},{48,32},{64,48},{80,64},{96,80},{112,96},{1... | collective-permute-start | bytes 786440 | tf_op jit(solution)/shard_map/ppermute | solution.py:451
  11.0 11.2 %collective-permute-start.3 = (bf16[128,1024]{1,0:T(8,128)(2,1)}, bf16[128,1024]{1,0:T(8,128)(2,1)S(1)}, u32[]{:S(2)}, u32[]{:S(2)}) collective-permute-start(bf16[128,1024]{1,0:T(8,128)(2,1)} %bitcast.61), channel_id=1, source_target_pairs={{0,16},{16,32},{32,48},{48,64},{64,80},{80,96},{96,112},{112,0},{1... | collective-permute-start | bytes 786440 | tf_op jit(solution)/shard_map/ppermute | solution.py:454
  23.0 14.2 %collective-permute-start.8 = (bf16[1024,128]{1,0:T(8,128)(2,1)}, bf16[1024,128]{1,0:T(8,128)(2,1)S(1)}, u32[]{:S(2)}, u32[]{:S(2)}) collective-permute-start(bf16[1024,128]{1,0:T(8,128)(2,1)} %get-tuple-element.40.refs_7_), channel_id=1, source_target_pairs={{0,16},{16,32},{32,48},{48,64},{64,80},{80,96},{96,112},{112,0},{1... | collective-permute-start | bytes 786440 | tf_op jit(solution)/shard_map/ppermute | solution.py:450
  23.0 14.3 %collective-permute-start.11 = (bf16[128,1024]{1,0:T(8,128)(2,1)}, bf16[128,1024]{1,0:T(8,128)(2,1)S(1)}, u32[]{:S(2)}, u32[]{:S(2)}) collective-permute-start(bf16[128,1024]{1,0:T(8,128)(2,1)} %get-tuple-element.41.refs_9_), channel_id=1, source_target_pairs={{0,112},{16,0},{32,16},{48,32},{64,48},{80,64},{96,80},{112,96},{1... | collective-permute-start | bytes 786440 | tf_op jit(solution)/shard_map/ppermute | solution.py:451
  25.6 14.3 %collective-permute-start.4 = (bf16[1024,128]{1,0:T(8,128)(2,1)}, bf16[1024,128]{1,0:T(8,128)(2,1)S(1)}, u32[]{:S(2)}, u32[]{:S(2)}) collective-permute-start(bf16[1024,128]{1,0:T(8,128)(2,1)} %get-tuple-element.37.refs_1_), channel_id=1, source_target_pairs={{0,112},{16,0},{32,16},{48,32},{64,48},{80,64},{96,80},{112,96},{1... | collective-permute-start | bytes 786440 | tf_op jit(solution)/shard_map/ppermute | solution.py:453
  25.7 14.4 %collective-permute-start.6 = (bf16[128,1024]{1,0:T(8,128)(2,1)}, bf16[128,1024]{1,0:T(8,128)(2,1)S(1)}, u32[]{:S(2)}, u32[]{:S(2)}) collective-permute-start(bf16[128,1024]{1,0:T(8,128)(2,1)} %get-tuple-element.38.refs_15_), channel_id=1, source_target_pairs={{0,16},{16,32},{32,48},{48,64},{64,80},{80,96},{96,112},{112,0},{1... | collective-permute-start | bytes 786440 | tf_op jit(solution)/shard_map/ppermute | solution.py:454
  27.1 31.0 %all-to-all-start = ((bf16[32,16,1024]{2,1,0:T(8,128)(2,1)}), bf16[32,16,1024]{2,1,0:T(8,128)(2,1)S(1)}, u32[]{:S(2)}, u32[]{:S(2)}) async-start(bf16[32,16,1024]{2,1,0:T(8,128)(2,1)} %bitcast.47), calls=%async_computation | async-start | bytes 2097152 | tf_op jit(solution)/shard_map/all_to_all | solution.py:466
  37.2 15.3 %copy-start.14 = (bf16[1024,128]{1,0:T(8,128)(2,1)}, bf16[1024,128]{1,0:T(8,128)(2,1)S(1)}, u32[]{:S(2)}) copy-start(bf16[1024,128]{1,0:T(8,128)(2,1)S(1)} %collective-permute-done.8.refs_6_) | copy-start | bytes 786436
  37.2 9.0 %collective-permute-start.9 = (bf16[1024,128]{1,0:T(8,128)(2,1)S(1)}, bf16[1024,128]{1,0:T(8,128)(2,1)S(1)}, u32[]{:S(2)}, u32[]{:S(2)}) collective-permute-start(bf16[1024,128]{1,0:T(8,128)(2,1)S(1)} %collective-permute-done.8.refs_6_), channel_id=1, source_target_pairs={{0,16},{16,32},{32,48},{48,64},{64,80},{80,96},{96,112},{112,0},{1... | collective-permute-start | bytes 786440 | tf_op jit(solution)/shard_map/ppermute | solution.py:450
  37.3 8.9 %collective-permute-start.12 = (bf16[128,1024]{1,0:T(8,128)(2,1)S(1)}, bf16[128,1024]{1,0:T(8,128)(2,1)S(1)}, u32[]{:S(2)}, u32[]{:S(2)}) collective-permute-start(bf16[128,1024]{1,0:T(8,128)(2,1)S(1)} %collective-permute-done.11.refs_10_), channel_id=1, source_target_pairs={{0,112},{16,0},{32,16},{48,32},{64,48},{80,64},{96,80},{112,96},{1... | collective-permute-start | bytes 786440 | tf_op jit(solution)/shard_map/ppermute | solution.py:451
  40.0 10.9 %collective-permute-start.5 = (bf16[1024,128]{1,0:T(8,128)(2,1)S(1)}, bf16[1024,128]{1,0:T(8,128)(2,1)S(1)}, u32[]{:S(2)}, u32[]{:S(2)}) collective-permute-start(bf16[1024,128]{1,0:T(8,128)(2,1)S(1)} %collective-permute-done.4.refs_2_), channel_id=1, source_target_pairs={{0,112},{16,0},{32,16},{48,32},{64,48},{80,64},{96,80},{112,96},{1... | collective-permute-start | bytes 786440 | tf_op jit(solution)/shard_map/ppermute | solution.py:453
  40.1 11.7 %collective-permute-start.7 = (bf16[128,1024]{1,0:T(8,128)(2,1)S(1)}, bf16[128,1024]{1,0:T(8,128)(2,1)S(1)}, u32[]{:S(2)}, u32[]{:S(2)}) collective-permute-start(bf16[128,1024]{1,0:T(8,128)(2,1)S(1)} %collective-permute-done.6.refs_14_), channel_id=1, source_target_pairs={{0,16},{16,32},{32,48},{48,64},{64,80},{80,96},{96,112},{112,0},{1... | collective-permute-start | bytes 786440 | tf_op jit(solution)/shard_map/ppermute | solution.py:454
  46.2 11.2 %collective-permute-start.10 = (bf16[1024,128]{1,0:T(8,128)(2,1)S(1)}, bf16[1024,128]{1,0:T(8,128)(2,1)S(1)}, u32[]{:S(2)}, u32[]{:S(2)}) collective-permute-start(bf16[1024,128]{1,0:T(8,128)(2,1)S(1)} %collective-permute-done.9.refs_5_), channel_id=1, source_target_pairs={{0,16},{16,32},{32,48},{48,64},{64,80},{80,96},{96,112},{112,0},{1... | collective-permute-start | bytes 786440 | tf_op jit(solution)/shard_map/ppermute | solution.py:450
  46.2 11.2 %collective-permute-start.13 = (bf16[128,1024]{1,0:T(8,128)(2,1)S(1)}, bf16[128,1024]{1,0:T(8,128)(2,1)}, u32[]{:S(2)}, u32[]{:S(2)}) collective-permute-start(bf16[128,1024]{1,0:T(8,128)(2,1)S(1)} %collective-permute-done.12.refs_11_), channel_id=1, source_target_pairs={{0,112},{16,0},{32,16},{48,32},{64,48},{80,64},{96,80},{112,96},{1... | collective-permute-start | bytes 786440 | tf_op jit(solution)/shard_map/ppermute | solution.py:451
  66.9 26.4 %copy-start.9 = (bf16[2048,128]{1,0:T(8,128)(2,1)S(1)}, bf16[2048,128]{1,0:T(8,128)(2,1)}, u32[]{:S(2)}) copy-start(bf16[2048,128]{1,0:T(8,128)(2,1)} %get-tuple-element.53) | copy-start | bytes 1572868
  67.0 27.3 %all-to-all-start.1 = ((bf16[32,16,1024]{2,1,0:T(8,128)(2,1)}), bf16[32,16,1024]{2,1,0:T(8,128)(2,1)S(1)}, u32[]{:S(2)}, u32[]{:S(2)}) async-start(bf16[32,16,1024]{2,1,0:T(8,128)(2,1)} %get-tuple-element.45), calls=%async_computation.1 | async-start | bytes 2097152 | tf_op jit(solution)/shard_map/all_to_all | solution.py:476
  75.2 13.6 %collective-permute-start.18 = (bf16[2048,128]{1,0:T(8,128)(2,1)}, bf16[2048,128]{1,0:T(8,128)(2,1)S(1)}, u32[]{:S(2)}, u32[]{:S(2)}) collective-permute-start(bf16[2048,128]{1,0:T(8,128)(2,1)} %get-tuple-element.54), channel_id=1, source_target_pairs={{0,112},{16,0},{32,16},{48,32},{64,48},{80,64},{96,80},{112,96},{1... | collective-permute-start | bytes 1572872 | tf_op jit(solution)/shard_map/ppermute | solution.py:483
  77.3 16.0 %collective-permute-start.16 = (bf16[2048,128]{1,0:T(8,128)(2,1)}, bf16[2048,128]{1,0:T(8,128)(2,1)S(1)}, u32[]{:S(2)}, u32[]{:S(2)}) collective-permute-start(bf16[2048,128]{1,0:T(8,128)(2,1)} %get-tuple-element.52), channel_id=1, source_target_pairs={{0,16},{16,32},{32,48},{48,64},{64,80},{80,96},{96,112},{112,0},{1... | collective-permute-start | bytes 1572872 | tf_op jit(solution)/shard_map/ppermute | solution.py:481
  89.9 18.2 %collective-permute-start.19 = (bf16[2048,128]{1,0:T(8,128)(2,1)S(1)}, bf16[2048,128]{1,0:T(8,128)(2,1)S(1)}, u32[]{:S(2)}, u32[]{:S(2)}) collective-permute-start(bf16[2048,128]{1,0:T(8,128)(2,1)S(1)} %add.22), channel_id=1, source_target_pairs={{0,112},{16,0},{32,16},{48,32},{64,48},{80,64},{96,80},{112,96},{1... | collective-permute-start | bytes 1572872 | tf_op jit(solution)/shard_map/ppermute | solution.py:483
  94.3 13.9 %collective-permute-start.17 = (bf16[2048,128]{1,0:T(8,128)(2,1)}, bf16[2048,128]{1,0:T(8,128)(2,1)S(1)}, u32[]{:S(2)}, u32[]{:S(2)}) collective-permute-start(bf16[2048,128]{1,0:T(8,128)(2,1)} %add.21), channel_id=1, source_target_pairs={{0,16},{16,32},{32,48},{48,64},{64,80},{80,96},{96,112},{112,0},{1... | collective-permute-start | bytes 1572872 | tf_op jit(solution)/shard_map/ppermute | solution.py:481
  95.3 20.6 %copy-start.7 = (bf16[2048,128]{1,0:T(8,128)(2,1)S(1)}, bf16[2048,128]{1,0:T(8,128)(2,1)}, u32[]{:S(2)}) copy-start(bf16[2048,128]{1,0:T(8,128)(2,1)} %get-tuple-element.60) | copy-start | bytes 1572868
  104.0 2.5 %collective-permute-start.14 = (f32[72,128]{1,0:T(8,128)}, f32[72,128]{1,0:T(8,128)S(1)}, u32[]{:S(2)}, u32[]{:S(2)}) collective-permute-start(f32[72,128]{1,0:T(8,128)} %get-tuple-element.48), channel_id=1, source_target_pairs={{0,1},{1,0},{2,3},{3,2},{4,5},{5,4},{6,7},{7,6},{8,9},{9,8},{10,11... | collective-permute-start | bytes 110600 | tf_op jit(solution)/shard_map/ppermute | solution.py:502
  107.3 15.4 %copy-start.6 = (bf16[2048,128]{1,0:T(8,128)(2,1)S(1)}, bf16[2048,128]{1,0:T(8,128)(2,1)}, u32[]{:S(2)}) copy-start(bf16[2048,128]{1,0:T(8,128)(2,1)} %get-tuple-element.58) | copy-start | bytes 1572868
  109.1 24.0 %copy-start.1 = (f32[1024]{0:T(1024)S(1)}, f32[1024]{0:T(1024)}, u32[]{:S(2)}) copy-start(f32[1024]{0:T(1024)} %copy.41) | copy-start | bytes 12292
  109.1 13.6 %collective-permute-start.20 = (bf16[2048,128]{1,0:T(8,128)(2,1)}, bf16[2048,128]{1,0:T(8,128)(2,1)}, u32[]{:S(2)}, u32[]{:S(2)}) collective-permute-start(bf16[2048,128]{1,0:T(8,128)(2,1)} %add.23), channel_id=1, source_target_pairs={{0,16},{16,32},{32,48},{48,64},{64,80},{80,96},{96,112},{112,0},{1... | collective-permute-start | bytes 1572872 | tf_op jit(solution)/shard_map/ppermute | solution.py:481
  109.1 17.3 %all-to-all-start.2 = ((f32[16,72,128]{2,1,0:T(8,128)}), f32[16,72,128]{2,1,0:T(8,128)S(1)}, u32[]{:S(2)}, u32[]{:S(2)}) async-start(f32[16,72,128]{2,1,0:T(8,128)} %add_up.3.refs_2_), calls=%async_computation.2 | async-start | bytes 1179648 | tf_op jit(solution)/shard_map/all_to_all | solution.py:504
  116.1 24.4 %collective-permute-start.22 = (bf16[2048,128]{1,0:T(8,128)(2,1)S(1)}, bf16[2048,128]{1,0:T(8,128)(2,1)S(1)}, u32[]{:S(2)}, u32[]{:S(2)}) collective-permute-start(bf16[2048,128]{1,0:T(8,128)(2,1)S(1)} %add.26), channel_id=1, source_target_pairs={{0,112},{16,0},{32,16},{48,32},{64,48},{80,64},{96,80},{112,96},{1... | collective-permute-start | bytes 1572872 | tf_op jit(solution)/shard_map/ppermute | solution.py:483
  124.7 15.8 %collective-permute-start.21 = (bf16[2048,128]{1,0:T(8,128)(2,1)}, bf16[2048,128]{1,0:T(8,128)(2,1)S(1)}, u32[]{:S(2)}, u32[]{:S(2)}) collective-permute-start(bf16[2048,128]{1,0:T(8,128)(2,1)} %add.24), channel_id=1, source_target_pairs={{0,16},{16,32},{32,48},{48,64},{64,80},{80,96},{96,112},{112,0},{1... | collective-permute-start | bytes 1572872 | tf_op jit(solution)/shard_map/ppermute | solution.py:481
  127.2 15.9 %all-to-all-start.3 = ((f32[8,72,128]{2,1,0:T(8,128)}), f32[8,72,128]{2,1,0:T(8,128)S(1)}, u32[]{:S(2)}, u32[]{:S(2)}) async-start(f32[8,72,128]{2,1,0:T(8,128)} %add_up.4.refs_1_), calls=%async_computation.3 | async-start | bytes 589824 | tf_op jit(solution)/shard_map/all_to_all | solution.py:511
  143.1 6.4 %collective-permute-start.15 = (f32[72,128]{1,0:T(8,128)S(1)}, f32[72,128]{1,0:T(8,128)S(1)}, u32[]{:S(2)}, u32[]{:S(2)}) collective-permute-start(f32[72,128]{1,0:T(8,128)S(1)} %bitcast.41), channel_id=1, source_target_pairs={{0,1},{1,0},{2,3},{3,2},{4,5},{5,4},{6,7},{7,6},{8,9},{9,8},{10,11... | collective-permute-start | bytes 110600 | tf_op jit(solution)/shard_map/ppermute | solution.py:516
  (18 other events, 86.2 us)

commit v4 on v3

--- a/solution.py
+++ b/solution.py
@@ -276,9 +276,34 @@
     )(*arrays)
 
 
+def finish_kernel(core_ref, mine_ref, other_ref, weight_ref, gain_ref):
+    slots, features = weight_ref.shape
+    part = mine_ref.shape[1]
+    blocks = features // part // 2
+    first = core_ref[0] == 0
+    mine, other = mine_ref[...], other_ref[...]
+    for k, rows in enumerate((jnp.where(first, mine, other), jnp.where(first, other, mine))):
+        for j in range(blocks):
+            here = slice((k * blocks + j) * part, (k * blocks + j + 1) * part)
+            weight_ref[:, here] = rows[j * slots : (j + 1) * slots]
+            gain_ref[:, here] = rows[blocks * slots + j : blocks * slots + j + 1]
+
+
+def finish(core, mine, other, slots, features):
+    return pl.pallas_call(
+        finish_kernel,
+        in_specs=[pl.BlockSpec(memory_space=pltpu.SMEM), vmem, vmem],
+        out_specs=[vmem] * 2,
+        out_shape=[jax.ShapeDtypeStruct((slots, features), f32), jax.ShapeDtypeStruct((1, features), f32)],
+        compiler_params=pltpu.CompilerParams(vmem_limit_bytes=8 * 1024 * 1024),
+        cost_estimate=pl.CostEstimate(flops=10**6, bytes_accessed=2**18, transcendentals=0),
+        name="finish",
+    )(core, mine, other)
+
+
 def route_kernel(
     shares, core_ref, gain_ref, slot_ref, col_ref, c_ref, normed_ref, ret_ref, acc_ref,
-    mine_ref, other_ref, coef_ref, grad_ref,
+    mine_ref, other_ref, gain_out, coef_ref, grad_ref,
     c_s, normed_s, ret_s, acc_s, coef_s, grad_s, out_s, pd_s, dd_s, fc_s,
     c_sem, normed_sem, whole_sem, coef_sem,
 ):
@@ -334,6 +359,7 @@
     part = mine_ref.shape[1]
     blocks = features // part // 2
     first = core_ref[0] == 0
+    gain_out[...] = gain_ref[...]
 
     def chosen(j, rows):
         low = rows[:, j * part : (j + 1) * part]
@@ -363,8 +389,8 @@
     return pl.pallas_call(
         functools.partial(route_kernel, shares),
         in_specs=[pl.BlockSpec(memory_space=pltpu.SMEM)] + [vmem] * 3 + [anywhere] * len(ins),
-        out_specs=[vmem] * 2 + [anywhere] * len(outs),
-        out_shape=[sums] * 2 + [jax.ShapeDtypeStruct(*out) for out in outs],
+        out_specs=[vmem] * 3 + [anywhere] * len(outs),
+        out_shape=[sums] * 2 + [jax.ShapeDtypeStruct(norm_gain.shape, f32)] + [jax.ShapeDtypeStruct(*out) for out in outs],
         scratch_shapes=[pltpu.VMEM(x.shape, x.dtype) for x in ins]
         + [pltpu.VMEM(*out) for out in outs]
         + [
@@ -496,7 +522,7 @@
     core = lax.axis_index("c")
     swap = [(0, 1), (1, 0)]
     ret = ret.reshape(halves, slots, 2 * images, features)
-    mine, other, coef, grad = route(core.reshape(1), cots, normed, gain, slot_t, col, ret, acc)
+    mine, other, late_gain, coef, grad = route(core.reshape(1), cots, normed, gain, slot_t, col, ret, acc)
     plane = ("yh", "yl", "x")
     n_plane = halves * lax.axis_size("yl") * lax.axis_size("x")
     copies = add_up([mine[None], lax.ppermute(other, "c", swap)[None]], n_plane)
@@ -506,7 +532,7 @@
         add_own(k)
         pass_on(k + 1)
     copies = add_up([copies], n)
-    (late_gain,) = after([gain], [copies], limit=LOW)
+    (late_gain,) = after([late_gain], [copies], limit=LOW)
     d_tokens = back(by_place, coef, late_gain, grad)
     (share,) = add_up([lax.all_to_all(copies, "z", 0, 0, tiled=True)], 1)
     pieces = features // part
@@ -514,11 +540,9 @@
     d_first = total[:features]
     d_second = total[features:].reshape(pieces, part, part).swapaxes(0, 1).reshape(part, features)
     other = lax.ppermute(share, "c", swap)
-    sums = jnp.stack([jnp.where(core == 0, share, other), jnp.where(core == 0, other, share)])
-    blocks = features // sums.shape[2] // 2
-    d_slot_weight = sums[:, : blocks * slots].reshape(2 * blocks, slots, -1)
-    d_slot_weight = d_slot_weight.swapaxes(0, 1).reshape(slots, features).T
-    d_gain = sums[:, blocks * slots : blocks * slots + blocks].reshape(features)
+    d_slot_weight, d_gain = finish(core.reshape(1), share, other, slots, features)
+    d_slot_weight = d_slot_weight.T
+    d_gain = d_gain.reshape(features)
     d_tokens = d_tokens.reshape(tok, images, features).swapaxes(0, 1)
     return (d_tokens, d_slot_weight, d_gain, d_first[None], d_second[None])
 

time: 152 us -> 150 us (0.987)
  local copies, waits for them, and re-layouts: 9.54 us -> 7.63 us
    unnamed x47 -> x46, local copies, waits for them, and re-layouts: 6.86 us -> 5.58 us
where the time goes in v4:
time: 150 us; the launch traced here: 149 us
  starting transfers between devices  65.7 us (44%)
  waiting for transfers between devices  34.9 us (23%)
  Pallas kernels  34.4 us (23%)
  local copies, waits for them, and re-layouts  7.63 us (5%)
  other arithmetic  5.36 us (4%)
    ppermute x3, waiting for transfers between devices, pass_on(): state[1] = lax.ppermute(state[1], 'z', down)  11.4 us
    ppermute x4, starting transfers between devices, step(): seconds[k] = lax.ppermute(seconds[k - 1], 'z', down)  10.7 us
    all_to_all x1, starting transfers between devices, on_device(): lax.all_to_all(sent.reshape(halves * slots, 2 * images, features), peers,...  10.1 us
    ppermute x4, waiting for transfers between devices, step(): firsts[n - k] = lax.ppermute(firsts[(n - k + 1) % n], 'z', up)  9.6 us
    pallas_call x1, Pallas kernels, front(): pl.pallas_call(functools.partial(front_kernel, shares), in_specs=[vmem, v...  8.77 us
    pallas_call x1, Pallas kernels, route(): pl.pallas_call(functools.partial(route_kernel, shares), in_specs=[pl.Bloc...  8.7 us
    ppermute x3, starting transfers between devices, pass_on(): state[1] = lax.ppermute(state[1], 'z', down)  8.55 us
    all_to_all x1, starting transfers between devices, on_device(): ret = lax.all_to_all(ret, peers, 0, 0, tiled=True)  8.21 us
  transfers between devices with their start and end apart: 27, of which 10 were waited for; matrix products, arithmetic and copies ran while one was open for 4% of the time, Pallas kernels for 17%

profile of v4, /device:TPU:1, one launch (start us, length us, event | category | flops | bytes accessed | tf_op | source)
XLA Modules:
  0.0 148.9 jit_solution(9260849732733257445)
XLA Ops:
  0.6 6.5 %collective-permute-start = (bf16[1024,128]{1,0:T(8,128)(2,1)}, bf16[1024,128]{1,0:T(8,128)(2,1)S(1)}, u32[]{:S(2)}, u32[]{:S(2)}) collective-permute-start(bf16[1024,128]{1,0:T(8,128)(2,1)} %bitcast.37), channel_id=1, source_target_pairs={{0,112},{16,0},{32,16},{48,32},{64,48},{80,64},{96,80},{112,96},{1... | collective-permute-start | bytes 786440 | tf_op jit(solution)/shard_map/ppermute | solution.py:479
  7.1 2.7 %collective-permute-start.2 = (bf16[128,1024]{1,0:T(8,128)(2,1)}, bf16[128,1024]{1,0:T(8,128)(2,1)S(1)}, u32[]{:S(2)}, u32[]{:S(2)}) collective-permute-start(bf16[128,1024]{1,0:T(8,128)(2,1)} %bitcast.40), channel_id=1, source_target_pairs={{0,112},{16,0},{32,16},{48,32},{64,48},{80,64},{96,80},{112,96},{1... | collective-permute-start | bytes 786440 | tf_op jit(solution)/shard_map/ppermute | solution.py:477
  9.8 8.8 %front.1 = (bf16[2,16,16,1024]{3,2,1,0:T(8,128)(2,1)}, bf16[1568,1024]{1,0:T(8,128)(2,1)}, f32[128,1024]{1,0:T(8,128)}, f32[8,128]{1,0:T(8,128)}) custom-call(f32[1,1024]{1,0:T(1,128)} %bitcast.46, bf16[16,1024]{1,0:T(8,128)(2,1)} %bitcast.44, bf16[1568,1024]{1,0:T(8,128)(2,1)} %bitcast.35, bf16[1568,1024]{1,0:T(8,128)(2,1)} %bitcast.33), custom_call_target="tpu_custom_call" | custom-call | flops 8000000000 | bytes 14680064 | tf_op jit(solution)/shard_map/front/pallas_call | solution.py:123
  18.6 2.4 %collective-permute-done.3.refs_4_ = bf16[128,1024]{1,0:T(8,128)(2,1)S(1)} collective-permute-done((bf16[128,1024]{1,0:T(8,128)(2,1)}, bf16[128,1024]{1,0:T(8,128)(2,1)S(1)}, u32[]{:S(2)}, u32[]{:S(2)}) %collective-permute-start.3) | collective-permute-done | bytes 262176 | tf_op jit(solution)/shard_map/ppermute | solution.py:480
  21.8 2.7 %collective-permute-start.11 = (bf16[128,1024]{1,0:T(8,128)(2,1)}, bf16[128,1024]{1,0:T(8,128)(2,1)S(1)}, u32[]{:S(2)}, u32[]{:S(2)}) collective-permute-start(bf16[128,1024]{1,0:T(8,128)(2,1)} %get-tuple-element.44.refs_9_), channel_id=1, source_target_pairs={{0,112},{16,0},{32,16},{48,32},{64,48},{80,64},{96,80},{112,96},{1... | collective-permute-start | bytes 786440 | tf_op jit(solution)/shard_map/ppermute | solution.py:477
  24.5 1.4 collective-permute-start.6
  25.9 10.1 %all-to-all-start = ((bf16[32,16,1024]{2,1,0:T(8,128)(2,1)}), bf16[32,16,1024]{2,1,0:T(8,128)(2,1)S(1)}, u32[]{:S(2)}, u32[]{:S(2)}) async-start(bf16[32,16,1024]{2,1,0:T(8,128)(2,1)} %bitcast.30), calls=%async_computation | async-start | bytes 2097152 | tf_op jit(solution)/shard_map/all_to_all | solution.py:492
  36.1 2.6 %collective-permute-start.12 = (bf16[128,1024]{1,0:T(8,128)(2,1)S(1)}, bf16[128,1024]{1,0:T(8,128)(2,1)S(1)}, u32[]{:S(2)}, u32[]{:S(2)}) collective-permute-start(bf16[128,1024]{1,0:T(8,128)(2,1)S(1)} %collective-permute-done.11.refs_10_), channel_id=1, source_target_pairs={{0,112},{16,0},{32,16},{48,32},{64,48},{80,64},{96,80},{112,96},{1... | collective-permute-start | bytes 786440 | tf_op jit(solution)/shard_map/ppermute | solution.py:477
  38.9 1.4 collective-permute-start.7
  40.2 4.7 %collective-permute-done.9.refs_5_ = bf16[1024,128]{1,0:T(8,128)(2,1)S(1)} collective-permute-done((bf16[1024,128]{1,0:T(8,128)(2,1)S(1)}, bf16[1024,128]{1,0:T(8,128)(2,1)S(1)}, u32[]{:S(2)}, u32[]{:S(2)}) %collective-permute-start.9) | collective-permute-done | bytes 262176 | tf_op jit(solution)/shard_map/ppermute | solution.py:476
  45.0 2.7 %collective-permute-start.13 = (bf16[128,1024]{1,0:T(8,128)(2,1)S(1)}, bf16[128,1024]{1,0:T(8,128)(2,1)}, u32[]{:S(2)}, u32[]{:S(2)}) collective-permute-start(bf16[128,1024]{1,0:T(8,128)(2,1)S(1)} %collective-permute-done.12.refs_11_), channel_id=1, source_target_pairs={{0,112},{16,0},{32,16},{48,32},{64,48},{80,64},{96,80},{112,96},{1... | collective-permute-start | bytes 786440 | tf_op jit(solution)/shard_map/ppermute | solution.py:477
  47.6 2.0 %collective-permute-done.5.refs_0_ = bf16[1024,128]{1,0:T(8,128)(2,1)S(1)} collective-permute-done((bf16[1024,128]{1,0:T(8,128)(2,1)S(1)}, bf16[1024,128]{1,0:T(8,128)(2,1)S(1)}, u32[]{:S(2)}, u32[]{:S(2)}) %collective-permute-start.5) | collective-permute-done | bytes 262176 | tf_op jit(solution)/shard_map/ppermute | solution.py:479
  51.3 4.9 %collective-permute-done.10.refs_0_ = bf16[1024,128]{1,0:T(8,128)(2,1)S(1)} collective-permute-done((bf16[1024,128]{1,0:T(8,128)(2,1)S(1)}, bf16[1024,128]{1,0:T(8,128)(2,1)S(1)}, u32[]{:S(2)}, u32[]{:S(2)}) %collective-permute-start.10) | collective-permute-done | bytes 262176 | tf_op jit(solution)/shard_map/ppermute | solution.py:476
  57.9 7.8 %expert.1 = (bf16[32,16,1024]{2,1,0:T(8,128)(2,1)}, bf16[2048,128]{1,0:T(8,128)(2,1)}, bf16[2048,128]{1,0:T(8,128)(2,1)}, bf16[2048,128]{1,0:T(8,128)(2,1)}, bf1...) custom-call(bf16[32,16,1024]{2,1,0:T(8,128)(2,1)} %copy-done.3, ...), custom_call_target="tpu_custom_call" | custom-call | flops 4000000000 | bytes 10485760 | tf_op jit(solution)/shard_map/expert/pallas_call | solution.py:231
  65.8 8.2 %all-to-all-start.1 = ((bf16[32,16,1024]{2,1,0:T(8,128)(2,1)}), bf16[32,16,1024]{2,1,0:T(8,128)(2,1)S(1)}, u32[]{:S(2)}, u32[]{:S(2)}) async-start(bf16[32,16,1024]{2,1,0:T(8,128)(2,1)} %get-tuple-element.48), calls=%async_computation.1 | async-start | bytes 2097152 | tf_op jit(solution)/shard_map/all_to_all | solution.py:502
  74.0 2.2 %collective-permute-start.18 = (bf16[2048,128]{1,0:T(8,128)(2,1)}, bf16[2048,128]{1,0:T(8,128)(2,1)S(1)}, u32[]{:S(2)}, u32[]{:S(2)}) collective-permute-start(bf16[2048,128]{1,0:T(8,128)(2,1)} %get-tuple-element.60), channel_id=1, source_target_pairs={{0,112},{16,0},{32,16},{48,32},{64,48},{80,64},{96,80},{112,96},{1... | collective-permute-start | bytes 1572872 | tf_op jit(solution)/shard_map/ppermute | solution.py:509
  76.1 11.4 %collective-permute-done.18 = bf16[2048,128]{1,0:T(8,128)(2,1)S(1)} collective-permute-done((bf16[2048,128]{1,0:T(8,128)(2,1)}, bf16[2048,128]{1,0:T(8,128)(2,1)S(1)}, u32[]{:S(2)}, u32[]{:S(2)}) %collective-permute-start.18) | collective-permute-done | bytes 524320 | tf_op jit(solution)/shard_map/ppermute | solution.py:509
  87.6 1.2 add.22
  88.7 3.4 %collective-permute-start.19 = (bf16[2048,128]{1,0:T(8,128)(2,1)S(1)}, bf16[2048,128]{1,0:T(8,128)(2,1)S(1)}, u32[]{:S(2)}, u32[]{:S(2)}) collective-permute-start(bf16[2048,128]{1,0:T(8,128)(2,1)S(1)} %add.22), channel_id=1, source_target_pairs={{0,112},{16,0},{32,16},{48,32},{64,48},{80,64},{96,80},{112,96},{1... | collective-permute-start | bytes 1572872 | tf_op jit(solution)/shard_map/ppermute | solution.py:509
  93.1 1.0 copy-done.4
  94.1 8.7 %route.1 = (f32[72,128]{1,0:T(8,128)}, f32[72,128]{1,0:T(8,128)}, f32[1,1024]{1,0:T(1,128)}, bf16[1568,256]{1,0:T(8,128)(2,1)}, bf16[256,1024]{1,0:T(8,128)(2,1)}) custom-call(s32[1]{0:T(128)} %bitcast.core_ref, f32[1,1024]{1,0:T(1,128)} %bitcast.47, bf16[16,1024]{1,0:T(8,128)(2,1)} %bitcast.45, f32[8,128]{1,0:T(8,128)} %get-tuple-element.36.col_ref, ...), custom_call_target="tpu_custom_call" | custom-call | flops 5000000000 | bytes 14680064 | tf_op jit(solution)/shard_map/route/pallas_call | solution.py:389
  102.8 1.4 collective-permute-start.14
  104.2 1.1 collective-permute-done.14
  107.9 6.7 %all-to-all-start.2 = ((f32[16,72,128]{2,1,0:T(8,128)}), f32[16,72,128]{2,1,0:T(8,128)S(1)}, u32[]{:S(2)}, u32[]{:S(2)}) async-start(f32[16,72,128]{2,1,0:T(8,128)} %add_up.3.refs_2_), calls=%async_computation.2 | async-start | bytes 1179648 | tf_op jit(solution)/shard_map/all_to_all | solution.py:530
  114.8 3.0 %collective-permute-start.22 = (bf16[2048,128]{1,0:T(8,128)(2,1)S(1)}, bf16[2048,128]{1,0:T(8,128)(2,1)S(1)}, u32[]{:S(2)}, u32[]{:S(2)}) collective-permute-start(bf16[2048,128]{1,0:T(8,128)(2,1)S(1)} %add.26), channel_id=1, source_target_pairs={{0,112},{16,0},{32,16},{48,32},{64,48},{80,64},{96,80},{112,96},{1... | collective-permute-start | bytes 1572872 | tf_op jit(solution)/shard_map/ppermute | solution.py:509
  117.8 3.7 %collective-permute-done.20 = bf16[2048,128]{1,0:T(8,128)(2,1)} collective-permute-done((bf16[2048,128]{1,0:T(8,128)(2,1)}, bf16[2048,128]{1,0:T(8,128)(2,1)}, u32[]{:S(2)}, u32[]{:S(2)}) %collective-permute-start.20) | collective-permute-done | bytes 524320 | tf_op jit(solution)/shard_map/ppermute | solution.py:507
  121.5 2.0 %add.24 = bf16[2048,128]{1,0:T(8,128)(2,1)} add(bf16[2048,128]{1,0:T(8,128)(2,1)} %collective-permute-done.20, bf16[2048,128]{1,0:T(8,128)(2,1)S(1)} %copy-done.6) | non-fusion elementwise | flops 262144 | bytes 1572864 | tf_op jit(solution)/shard_map/add | solution.py:512
  123.5 1.6 %all-to-all-done.2.refs_0_ = f32[16,72,128]{2,1,0:T(8,128)S(1)} async-done(((f32[16,72,128]{2,1,0:T(8,128)}), f32[16,72,128]{2,1,0:T(8,128)S(1)}, u32[]{:S(2)}, u32[]{:S(2)}) %all-to-all-start.2) | async-done | bytes 589856 | tf_op jit(solution)/shard_map/all_to_all | solution.py:530
  125.9 6.0 %all-to-all-start.3 = ((f32[8,72,128]{2,1,0:T(8,128)}), f32[8,72,128]{2,1,0:T(8,128)S(1)}, u32[]{:S(2)}, u32[]{:S(2)}) async-start(f32[8,72,128]{2,1,0:T(8,128)} %add_up.4.refs_1_), calls=%async_computation.3 | async-start | bytes 589824 | tf_op jit(solution)/shard_map/all_to_all | solution.py:537
  132.5 6.8 %back.1 = bf16[1568,1024]{1,0:T(8,128)(2,1)} custom-call(f32[1,1024]{1,0:T(1,128)} %copy-done.2, bf16[256,1024]{1,0:T(8,128)(2,1)} %get-tuple-element.53.grad_ref, bf16[1568,1024]{1,0:T(8,128)(2,1)} %bitcast.36, bf16[1568,256]{1,0:T(8,128)(2,1)} %get-tuple-element.54.coef_ref), custom_call_target="tpu_custom_call" | custom-call | flops 5000000000 | bytes 8388608 | tf_op jit(solution)/shard_map/back/pallas_call | solution.py:428
  139.5 2.1 %all-to-all-done.3.refs_0_ = f32[8,72,128]{2,1,0:T(8,128)S(1)} async-done(((f32[8,72,128]{2,1,0:T(8,128)}), f32[8,72,128]{2,1,0:T(8,128)S(1)}, u32[]{:S(2)}, u32[]{:S(2)}) %all-to-all-start.3) | async-done | bytes 294944 | tf_op jit(solution)/shard_map/all_to_all | solution.py:537
  141.7 4.5 %collective-permute-start.15 = (f32[72,128]{1,0:T(8,128)S(1)}, f32[72,128]{1,0:T(8,128)S(1)}, u32[]{:S(2)}, u32[]{:S(2)}) collective-permute-start(f32[72,128]{1,0:T(8,128)S(1)} %bitcast.26), channel_id=1, source_target_pairs={{0,1},{1,0},{2,3},{3,2},{4,5},{5,4},{6,7},{7,6},{8,9},{9,8},{10,11... | collective-permute-start | bytes 110600 | tf_op jit(solution)/shard_map/ppermute | solution.py:542
  (90 shorter events, 12.3 us)
Async XLA Ops:
  0.6 17.9 %collective-permute-start = (bf16[1024,128]{1,0:T(8,128)(2,1)}, bf16[1024,128]{1,0:T(8,128)(2,1)S(1)}, u32[]{:S(2)}, u32[]{:S(2)}) collective-permute-start(bf16[1024,128]{1,0:T(8,128)(2,1)} %bitcast.37), channel_id=1, source_target_pairs={{0,112},{16,0},{32,16},{48,32},{64,48},{80,64},{96,80},{112,96},{1... | collective-permute-start | bytes 786440 | tf_op jit(solution)/shard_map/ppermute | solution.py:479
  7.1 11.5 %collective-permute-start.1 = (bf16[1024,128]{1,0:T(8,128)(2,1)}, bf16[1024,128]{1,0:T(8,128)(2,1)S(1)}, u32[]{:S(2)}, u32[]{:S(2)}) collective-permute-start(bf16[1024,128]{1,0:T(8,128)(2,1)} %bitcast.38), channel_id=1, source_target_pairs={{0,16},{16,32},{32,48},{48,64},{64,80},{80,96},{96,112},{112,0},{1... | collective-permute-start | bytes 786440 | tf_op jit(solution)/shard_map/ppermute | solution.py:476
  7.1 11.5 %collective-permute-start.2 = (bf16[128,1024]{1,0:T(8,128)(2,1)}, bf16[128,1024]{1,0:T(8,128)(2,1)S(1)}, u32[]{:S(2)}, u32[]{:S(2)}) collective-permute-start(bf16[128,1024]{1,0:T(8,128)(2,1)} %bitcast.40), channel_id=1, source_target_pairs={{0,112},{16,0},{32,16},{48,32},{64,48},{80,64},{96,80},{112,96},{1... | collective-permute-start | bytes 786440 | tf_op jit(solution)/shard_map/ppermute | solution.py:477
  9.8 11.2 %collective-permute-start.3 = (bf16[128,1024]{1,0:T(8,128)(2,1)}, bf16[128,1024]{1,0:T(8,128)(2,1)S(1)}, u32[]{:S(2)}, u32[]{:S(2)}) collective-permute-start(bf16[128,1024]{1,0:T(8,128)(2,1)} %bitcast.41), channel_id=1, source_target_pairs={{0,16},{16,32},{32,48},{48,64},{64,80},{80,96},{96,112},{112,0},{1... | collective-permute-start | bytes 786440 | tf_op jit(solution)/shard_map/ppermute | solution.py:480
  21.7 14.2 %collective-permute-start.8 = (bf16[1024,128]{1,0:T(8,128)(2,1)}, bf16[1024,128]{1,0:T(8,128)(2,1)S(1)}, u32[]{:S(2)}, u32[]{:S(2)}) collective-permute-start(bf16[1024,128]{1,0:T(8,128)(2,1)} %get-tuple-element.43.refs_7_), channel_id=1, source_target_pairs={{0,16},{16,32},{32,48},{48,64},{64,80},{80,96},{96,112},{112,0},{1... | collective-permute-start | bytes 786440 | tf_op jit(solution)/shard_map/ppermute | solution.py:476
  21.8 14.3 %collective-permute-start.11 = (bf16[128,1024]{1,0:T(8,128)(2,1)}, bf16[128,1024]{1,0:T(8,128)(2,1)S(1)}, u32[]{:S(2)}, u32[]{:S(2)}) collective-permute-start(bf16[128,1024]{1,0:T(8,128)(2,1)} %get-tuple-element.44.refs_9_), channel_id=1, source_target_pairs={{0,112},{16,0},{32,16},{48,32},{64,48},{80,64},{96,80},{112,96},{1... | collective-permute-start | bytes 786440 | tf_op jit(solution)/shard_map/ppermute | solution.py:477
  24.4 14.3 %collective-permute-start.4 = (bf16[1024,128]{1,0:T(8,128)(2,1)}, bf16[1024,128]{1,0:T(8,128)(2,1)S(1)}, u32[]{:S(2)}, u32[]{:S(2)}) collective-permute-start(bf16[1024,128]{1,0:T(8,128)(2,1)} %get-tuple-element.40.refs_1_), channel_id=1, source_target_pairs={{0,112},{16,0},{32,16},{48,32},{64,48},{80,64},{96,80},{112,96},{1... | collective-permute-start | bytes 786440 | tf_op jit(solution)/shard_map/ppermute | solution.py:479
  24.5 14.4 %collective-permute-start.6 = (bf16[128,1024]{1,0:T(8,128)(2,1)}, bf16[128,1024]{1,0:T(8,128)(2,1)S(1)}, u32[]{:S(2)}, u32[]{:S(2)}) collective-permute-start(bf16[128,1024]{1,0:T(8,128)(2,1)} %get-tuple-element.41.refs_15_), channel_id=1, source_target_pairs={{0,16},{16,32},{32,48},{48,64},{64,80},{80,96},{96,112},{112,0},{1... | collective-permute-start | bytes 786440 | tf_op jit(solution)/shard_map/ppermute | solution.py:480
  25.9 31.0 %all-to-all-start = ((bf16[32,16,1024]{2,1,0:T(8,128)(2,1)}), bf16[32,16,1024]{2,1,0:T(8,128)(2,1)S(1)}, u32[]{:S(2)}, u32[]{:S(2)}) async-start(bf16[32,16,1024]{2,1,0:T(8,128)(2,1)} %bitcast.30), calls=%async_computation | async-start | bytes 2097152 | tf_op jit(solution)/shard_map/all_to_all | solution.py:492
  36.0 15.3 %copy-start.14 = (bf16[1024,128]{1,0:T(8,128)(2,1)}, bf16[1024,128]{1,0:T(8,128)(2,1)S(1)}, u32[]{:S(2)}) copy-start(bf16[1024,128]{1,0:T(8,128)(2,1)S(1)} %collective-permute-done.8.refs_6_) | copy-start | bytes 786436
  36.0 9.0 %collective-permute-start.9 = (bf16[1024,128]{1,0:T(8,128)(2,1)S(1)}, bf16[1024,128]{1,0:T(8,128)(2,1)S(1)}, u32[]{:S(2)}, u32[]{:S(2)}) collective-permute-start(bf16[1024,128]{1,0:T(8,128)(2,1)S(1)} %collective-permute-done.8.refs_6_), channel_id=1, source_target_pairs={{0,16},{16,32},{32,48},{48,64},{64,80},{80,96},{96,112},{112,0},{1... | collective-permute-start | bytes 786440 | tf_op jit(solution)/shard_map/ppermute | solution.py:476
  36.1 8.9 %collective-permute-start.12 = (bf16[128,1024]{1,0:T(8,128)(2,1)S(1)}, bf16[128,1024]{1,0:T(8,128)(2,1)S(1)}, u32[]{:S(2)}, u32[]{:S(2)}) collective-permute-start(bf16[128,1024]{1,0:T(8,128)(2,1)S(1)} %collective-permute-done.11.refs_10_), channel_id=1, source_target_pairs={{0,112},{16,0},{32,16},{48,32},{64,48},{80,64},{96,80},{112,96},{1... | collective-permute-start | bytes 786440 | tf_op jit(solution)/shard_map/ppermute | solution.py:477
  38.8 10.9 %collective-permute-start.5 = (bf16[1024,128]{1,0:T(8,128)(2,1)S(1)}, bf16[1024,128]{1,0:T(8,128)(2,1)S(1)}, u32[]{:S(2)}, u32[]{:S(2)}) collective-permute-start(bf16[1024,128]{1,0:T(8,128)(2,1)S(1)} %collective-permute-done.4.refs_2_), channel_id=1, source_target_pairs={{0,112},{16,0},{32,16},{48,32},{64,48},{80,64},{96,80},{112,96},{1... | collective-permute-start | bytes 786440 | tf_op jit(solution)/shard_map/ppermute | solution.py:479
  38.9 11.7 %collective-permute-start.7 = (bf16[128,1024]{1,0:T(8,128)(2,1)S(1)}, bf16[128,1024]{1,0:T(8,128)(2,1)S(1)}, u32[]{:S(2)}, u32[]{:S(2)}) collective-permute-start(bf16[128,1024]{1,0:T(8,128)(2,1)S(1)} %collective-permute-done.6.refs_14_), channel_id=1, source_target_pairs={{0,16},{16,32},{32,48},{48,64},{64,80},{80,96},{96,112},{112,0},{1... | collective-permute-start | bytes 786440 | tf_op jit(solution)/shard_map/ppermute | solution.py:480
  45.0 11.2 %collective-permute-start.10 = (bf16[1024,128]{1,0:T(8,128)(2,1)S(1)}, bf16[1024,128]{1,0:T(8,128)(2,1)S(1)}, u32[]{:S(2)}, u32[]{:S(2)}) collective-permute-start(bf16[1024,128]{1,0:T(8,128)(2,1)S(1)} %collective-permute-done.9.refs_5_), channel_id=1, source_target_pairs={{0,16},{16,32},{32,48},{48,64},{64,80},{80,96},{96,112},{112,0},{1... | collective-permute-start | bytes 786440 | tf_op jit(solution)/shard_map/ppermute | solution.py:476
  45.0 11.2 %collective-permute-start.13 = (bf16[128,1024]{1,0:T(8,128)(2,1)S(1)}, bf16[128,1024]{1,0:T(8,128)(2,1)}, u32[]{:S(2)}, u32[]{:S(2)}) collective-permute-start(bf16[128,1024]{1,0:T(8,128)(2,1)S(1)} %collective-permute-done.12.refs_11_), channel_id=1, source_target_pairs={{0,112},{16,0},{32,16},{48,32},{64,48},{80,64},{96,80},{112,96},{1... | collective-permute-start | bytes 786440 | tf_op jit(solution)/shard_map/ppermute | solution.py:477
  65.7 26.4 %copy-start.9 = (bf16[2048,128]{1,0:T(8,128)(2,1)S(1)}, bf16[2048,128]{1,0:T(8,128)(2,1)}, u32[]{:S(2)}) copy-start(bf16[2048,128]{1,0:T(8,128)(2,1)} %get-tuple-element.59) | copy-start | bytes 1572868
  65.8 27.3 %all-to-all-start.1 = ((bf16[32,16,1024]{2,1,0:T(8,128)(2,1)}), bf16[32,16,1024]{2,1,0:T(8,128)(2,1)S(1)}, u32[]{:S(2)}, u32[]{:S(2)}) async-start(bf16[32,16,1024]{2,1,0:T(8,128)(2,1)} %get-tuple-element.48), calls=%async_computation.1 | async-start | bytes 2097152 | tf_op jit(solution)/shard_map/all_to_all | solution.py:502
  74.0 13.6 %collective-permute-start.18 = (bf16[2048,128]{1,0:T(8,128)(2,1)}, bf16[2048,128]{1,0:T(8,128)(2,1)S(1)}, u32[]{:S(2)}, u32[]{:S(2)}) collective-permute-start(bf16[2048,128]{1,0:T(8,128)(2,1)} %get-tuple-element.60), channel_id=1, source_target_pairs={{0,112},{16,0},{32,16},{48,32},{64,48},{80,64},{96,80},{112,96},{1... | collective-permute-start | bytes 1572872 | tf_op jit(solution)/shard_map/ppermute | solution.py:509
  76.1 16.0 %collective-permute-start.16 = (bf16[2048,128]{1,0:T(8,128)(2,1)}, bf16[2048,128]{1,0:T(8,128)(2,1)S(1)}, u32[]{:S(2)}, u32[]{:S(2)}) collective-permute-start(bf16[2048,128]{1,0:T(8,128)(2,1)} %get-tuple-element.58), channel_id=1, source_target_pairs={{0,16},{16,32},{32,48},{48,64},{64,80},{80,96},{96,112},{112,0},{1... | collective-permute-start | bytes 1572872 | tf_op jit(solution)/shard_map/ppermute | solution.py:507
  88.7 18.2 %collective-permute-start.19 = (bf16[2048,128]{1,0:T(8,128)(2,1)S(1)}, bf16[2048,128]{1,0:T(8,128)(2,1)S(1)}, u32[]{:S(2)}, u32[]{:S(2)}) collective-permute-start(bf16[2048,128]{1,0:T(8,128)(2,1)S(1)} %add.22), channel_id=1, source_target_pairs={{0,112},{16,0},{32,16},{48,32},{64,48},{80,64},{96,80},{112,96},{1... | collective-permute-start | bytes 1572872 | tf_op jit(solution)/shard_map/ppermute | solution.py:509
  93.1 13.9 %collective-permute-start.17 = (bf16[2048,128]{1,0:T(8,128)(2,1)}, bf16[2048,128]{1,0:T(8,128)(2,1)S(1)}, u32[]{:S(2)}, u32[]{:S(2)}) collective-permute-start(bf16[2048,128]{1,0:T(8,128)(2,1)} %add.21), channel_id=1, source_target_pairs={{0,16},{16,32},{32,48},{48,64},{64,80},{80,96},{96,112},{112,0},{1... | collective-permute-start | bytes 1572872 | tf_op jit(solution)/shard_map/ppermute | solution.py:507
  94.1 20.5 %copy-start.7 = (bf16[2048,128]{1,0:T(8,128)(2,1)S(1)}, bf16[2048,128]{1,0:T(8,128)(2,1)}, u32[]{:S(2)}) copy-start(bf16[2048,128]{1,0:T(8,128)(2,1)} %get-tuple-element.66) | copy-start | bytes 1572868
  102.8 2.5 %collective-permute-start.14 = (f32[72,128]{1,0:T(8,128)}, f32[72,128]{1,0:T(8,128)S(1)}, u32[]{:S(2)}, u32[]{:S(2)}) collective-permute-start(f32[72,128]{1,0:T(8,128)} %get-tuple-element.52), channel_id=1, source_target_pairs={{0,1},{1,0},{2,3},{3,2},{4,5},{5,4},{6,7},{7,6},{8,9},{9,8},{10,11... | collective-permute-start | bytes 110600 | tf_op jit(solution)/shard_map/ppermute | solution.py:528
  106.1 15.4 %copy-start.6 = (bf16[2048,128]{1,0:T(8,128)(2,1)S(1)}, bf16[2048,128]{1,0:T(8,128)(2,1)}, u32[]{:S(2)}) copy-start(bf16[2048,128]{1,0:T(8,128)(2,1)} %get-tuple-element.64) | copy-start | bytes 1572868
  107.9 24.0 %copy-start.1 = (f32[1,1024]{1,0:T(1,128)S(1)}, f32[1,1024]{1,0:T(1,128)}, u32[]{:S(2)}) copy-start(f32[1,1024]{1,0:T(1,128)} %get-tuple-element.50.refs_0_) | copy-start | bytes 12292
  107.9 13.6 %collective-permute-start.20 = (bf16[2048,128]{1,0:T(8,128)(2,1)}, bf16[2048,128]{1,0:T(8,128)(2,1)}, u32[]{:S(2)}, u32[]{:S(2)}) collective-permute-start(bf16[2048,128]{1,0:T(8,128)(2,1)} %add.23), channel_id=1, source_target_pairs={{0,16},{16,32},{32,48},{48,64},{64,80},{80,96},{96,112},{112,0},{1... | collective-permute-start | bytes 1572872 | tf_op jit(solution)/shard_map/ppermute | solution.py:507
  107.9 17.2 %all-to-all-start.2 = ((f32[16,72,128]{2,1,0:T(8,128)}), f32[16,72,128]{2,1,0:T(8,128)S(1)}, u32[]{:S(2)}, u32[]{:S(2)}) async-start(f32[16,72,128]{2,1,0:T(8,128)} %add_up.3.refs_2_), calls=%async_computation.2 | async-start | bytes 1179648 | tf_op jit(solution)/shard_map/all_to_all | solution.py:530
  114.8 24.5 %collective-permute-start.22 = (bf16[2048,128]{1,0:T(8,128)(2,1)S(1)}, bf16[2048,128]{1,0:T(8,128)(2,1)S(1)}, u32[]{:S(2)}, u32[]{:S(2)}) collective-permute-start(bf16[2048,128]{1,0:T(8,128)(2,1)S(1)} %add.26), channel_id=1, source_target_pairs={{0,112},{16,0},{32,16},{48,32},{64,48},{80,64},{96,80},{112,96},{1... | collective-permute-start | bytes 1572872 | tf_op jit(solution)/shard_map/ppermute | solution.py:509
  123.5 15.8 %collective-permute-start.21 = (bf16[2048,128]{1,0:T(8,128)(2,1)}, bf16[2048,128]{1,0:T(8,128)(2,1)S(1)}, u32[]{:S(2)}, u32[]{:S(2)}) collective-permute-start(bf16[2048,128]{1,0:T(8,128)(2,1)} %add.24), channel_id=1, source_target_pairs={{0,16},{16,32},{32,48},{48,64},{64,80},{80,96},{96,112},{112,0},{1... | collective-permute-start | bytes 1572872 | tf_op jit(solution)/shard_map/ppermute | solution.py:507
  125.9 15.8 %all-to-all-start.3 = ((f32[8,72,128]{2,1,0:T(8,128)}), f32[8,72,128]{2,1,0:T(8,128)S(1)}, u32[]{:S(2)}, u32[]{:S(2)}) async-start(f32[8,72,128]{2,1,0:T(8,128)} %add_up.4.refs_1_), calls=%async_computation.3 | async-start | bytes 589824 | tf_op jit(solution)/shard_map/all_to_all | solution.py:537
  141.7 6.6 %collective-permute-start.15 = (f32[72,128]{1,0:T(8,128)S(1)}, f32[72,128]{1,0:T(8,128)S(1)}, u32[]{:S(2)}, u32[]{:S(2)}) collective-permute-start(f32[72,128]{1,0:T(8,128)S(1)} %bitcast.26), channel_id=1, source_target_pairs={{0,1},{1,0},{2,3},{3,2},{4,5},{5,4},{6,7},{7,6},{8,9},{9,8},{10,11... | collective-permute-start | bytes 110600 | tf_op jit(solution)/shard_map/ppermute | solution.py:542
  (18 other events, 86.2 us)
